TPU v7x, 128 devices: a whole 4x4x4 slice. The times are simulated.
128 devices in a mesh: row: 16 (over x_hi, z, core), col: 8 (over x_lo, y).
Axes of the slice: x: 4 (x_hi: 2, x_lo: 2; x = x_hi * 2 + x_lo), y: 4, z: 4, core: 2. Of those that a mesh axis runs over, the one named last changes fastest.
Arguments:
- pair: bfloat16 [1024, 1024, 128], P('row', 'col'), may hold values from -6 to 6
- in_gain: float32 [128], replicated, may hold values from 0.25 to 1.75
- in_bias: float32 [128], replicated, may hold values from -3 to 3
- w_proj: bfloat16 [128, 128], replicated, may hold values from -0.5 to 0.5
- w_gate: bfloat16 [128, 128], replicated, may hold values from -0.5 to 0.5
- w_out_gate: bfloat16 [128, 128], replicated, may hold values from -0.5 to 0.5
- out_gain: float32 [64], replicated, may hold values from 0.25 to 1.75
- out_bias: float32 [64], replicated, may hold values from -3 to 3
- w_out: bfloat16 [64, 128], replicated, may hold values from -0.75 to 0.75
Outputs:
- update: bfloat16 [1024, 1024, 128], P('row', 'col')
All inputs are finite; a program needn't handle non-finite values.
Results may differ from a plain program's by a relative error of at most 0.018.
Values may be sent and summed in bfloat16 or wider, within the bound.
No kernel may reach another device: no remote copies, remote signals or barrier semaphores. Data moves between devices by JAX's collectives and lax.ppermute only.
A program may use at most 128 MiB of HBM per device.

v0:
```python
import jax
import jax.numpy as jnp
from jax import lax
from jax.sharding import PartitionSpec as P


def normalize(values, gain, bias):
    mean = jnp.mean(values, axis=-1, keepdims=True)
    centered = values - mean
    var = jnp.mean(centered * centered, axis=-1, keepdims=True)
    return centered * lax.rsqrt(var + 1e-05) * gain + bias


def local(pair, in_gain, in_bias, w_proj, w_gate, w_out_gate, out_gain, out_bias, w_out):
    rows_here, cols_here, channels = pair.shape
    hidden = w_out.shape[0]
    normed = normalize(pair.astype(jnp.float32), in_gain, in_bias).astype(jnp.bfloat16)
    flat = normed.reshape(-1, channels)
    proj = jnp.dot(flat, w_proj, preferred_element_type=jnp.float32)
    gates = jnp.dot(flat, w_gate, preferred_element_type=jnp.float32)
    both = (
        (jax.nn.sigmoid(gates) * proj)
        .astype(jnp.bfloat16)
        .reshape(rows_here, cols_here, 2 * hidden)
    )
    a_side = jnp.transpose(both[:, :, :hidden], (2, 0, 1))
    b_lead = jnp.transpose(both[:, :, hidden:], (0, 2, 1))
    b_every = lax.all_gather(b_lead, "row", axis=0, tiled=True)
    summed = lax.psum_scatter(
        jnp.einsum("jck,cik->jci", b_every, a_side, preferred_element_type=jnp.float32).astype(
            jnp.bfloat16
        ),
        "col",
        scatter_dimension=0,
        tiled=True,
    ).astype(jnp.float32)
    mixed = jnp.transpose(summed, (2, 0, 1))
    mixed_normed = normalize(mixed, out_gain, out_bias).astype(jnp.bfloat16)
    projected = jnp.dot(mixed_normed.reshape(-1, hidden), w_out, preferred_element_type=jnp.float32)
    out_gates = jax.nn.sigmoid(jnp.dot(flat, w_out_gate, preferred_element_type=jnp.float32))
    update = (out_gates * projected).astype(jnp.bfloat16)
    return update.reshape(rows_here, cols_here, channels)


def solution(mesh):
    return jax.shard_map(
        local,
        mesh=mesh,
        in_specs=(P("row", "col", None), P(), P(), P(), P(), P(), P(), P(), P()),
        out_specs=P("row", "col", None),
        check_vma=False,
    )
```

profile of v0, /device:TPU:0, one launch (start us, length us, event | category | flops | bytes accessed | tf_op | source)
XLA Modules:
  0.0 261.7 jit_solution(12793082269486598803)
XLA Ops:
  6.5 0.0 copy-start
  6.5 0.0 copy-start.1
  6.5 0.0 copy-start.8
  6.5 0.0 copy-start.7
  6.5 0.0 all-gather.2.cloned.1.call-start
  6.6 2.4 convert_reduce_fusion
  9.0 3.6 %fusion.10 = f32[64,128]{1,0:T(8,128)S(1)} fusion(bf16[64,128,128]{2,1,0:T(8,128)(2,1)} %param.9, f32[64,128]{1,0:T(8,128)S(1)} %broadcast_multiply_fusion.1), kind=kLoop, calls=%fused_computation.17 | loop fusion | flops 4186112 | bytes 2162688 | tf_op jit(solution)/shard_map/reduce_sum | solution.py:10
  12.6 0.0 copy-done.1
  12.6 0.0 copy-done.8
  12.6 0.0 copy-done.7
  12.6 2.5 fusion.13
  15.1 0.0 copy-start.2
  15.1 0.0 copy-done
  15.1 0.0 copy-start.5
  15.1 1.3 fusion.7
  16.4 0.0 copy-done.2
  16.4 0.0 copy-done.5
  16.4 0.7 fusion.4
  17.1 2.3 fusion.23
  19.5 3.4 %copy.19 = bf16[64,128,64]{1,0,2:T(8,128)(2,1)} copy(bf16[64,128,64]{2,1,0:T(8,128)(2,1)} %get-tuple-element.6) | data formatting | bytes 2097152
  22.9 0.0 all-gather.2.cloned.1.call-update
  22.9 0.2 reduce-scatter.4.cloned.1.call-start
  23.2 1.7 copy.18
  24.9 110.1 %all-gather.2.cloned.1.call-done = bf16[1024,64,128]{2,0,1:T(8,128)(2,1)} async-done(((bf16[64,64,128]{2,0,1:T(8,128)(2,1)}), bf16[1024,64,128]{2,0,1:T(8,128)(2,1)}) %all-gather.2.cloned.1.call-update) | async-done | bytes 16777232 | tf_op jit(solution)/shard_map/all_gather | solution.py:28
  134.9 11.4 %convolution_convert_fusion = bf16[64,64,1024]{2,1,0:T(8,128)(2,1)} fusion(bf16[1024,64,128]{2,0,1:T(8,128)(2,1)} %all-gather.2.cloned.1.call-done, bf16[64,128,64]{1,0,2:T(8,128)(2,1)S(1)} %copy.18), kind=kOutput, calls=%fused_computation.12 | convolution fusion | flops 1077936128 | bytes 26214400 | tf_op jit(solution)/shard_map/jck,cik->jci/dot_general | solution.py:30
  146.3 11.8 %copy.16 = bf16[1024,4096]{1,0:T(8,128)(2,1)} copy(bf16[1024,4096]{0,1:T(8,128)(2,1)} %bitcast.42) | data formatting | bytes 16777216
  158.1 0.0 copy-start.3
  158.1 0.0 copy-start.11
  158.1 0.0 reduce-scatter.4.cloned.1.call-update
  158.2 1.6 copy-done.3
  159.7 0.0 copy-done.11
  159.7 3.2 %fusion.6 = f32[8192,128]{1,0:T(8,128)} fusion(bf16[8192,128]{1,0:T(8,128)(2,1)S(1)} %bitcast.48, bf16[128,128]{1,0:T(8,128)(2,1)S(1)} %copy-done.11), kind=kOutput, calls=%fused_computation.10 | convolution fusion | flops 271581184 | bytes 6324224 | tf_op jit(solution)/shard_map/dot_general | solution.py:40
  162.9 0.0 copy-start.9
  162.9 0.0 copy-start.10
  162.9 0.0 copy-start.6
  162.9 85.7 %reduce-scatter.4.cloned.1.call-done = bf16[128,4096]{1,0:T(8,128)(2,1)} async-done(((bf16[1024,4096]{1,0:T(8,128)(2,1)}), bf16[128,4096]{1,0:T(8,128)(2,1)}) %reduce-scatter.4.cloned.1.call-update) | async-done | bytes 1048592
  248.6 1.6 copy.17
  250.2 0.0 copy-start.4
  250.2 0.2 bitcast_reduce_fusion
  250.4 0.3 fusion.16
  250.7 0.0 copy-done.9
  250.7 0.0 copy-done.10
  250.7 0.5 fusion.19
  251.2 0.0 copy-done.6
  251.2 1.2 copy-done.4
  252.4 2.5 fusion.5
  (4 shorter events, 0.0 us)
Async XLA Ops:
  6.5 8.6 %copy-start = (bf16[128,128]{1,0:T(8,128)(2,1)S(1)}, bf16[128,128]{1,0:T(8,128)(2,1)}, u32[]{:S(2)}) copy-start(bf16[128,128]{1,0:T(8,128)(2,1)} %param.13) | copy-start | bytes 98308
  6.5 6.0 %copy-start.1 = (bf16[64,128,128]{2,1,0:T(8,128)(2,1)S(1)}, bf16[64,128,128]{2,1,0:T(8,128)(2,1)}, u32[]{:S(2)}) copy-start(bf16[64,128,128]{2,1,0:T(8,128)(2,1)} %param.9) | copy-start | bytes 6291460
  6.5 6.0 %copy-start.8 = (f32[128]{0:T(128)S(1)}, f32[128]{0:T(128)}, u32[]{:S(2)}) copy-start(f32[128]{0:T(128)} %param.10) | copy-start | bytes 1540
  6.5 6.0 %copy-start.7 = (f32[128]{0:T(128)S(1)}, f32[128]{0:T(128)}, u32[]{:S(2)}) copy-start(f32[128]{0:T(128)} %param.11) | copy-start | bytes 1540
  6.5 128.4 %all-gather.2.cloned.1.call-start = ((), (), s32[]{:S(2)}) async-start(), calls=%async_computation.1 | async-start | bytes 17825792 | tf_op jit(solution)/shard_map/all_gather | solution.py:28
  15.1 1.3 copy-start.2
  15.1 1.3 copy-start.5
  22.9 225.7 %reduce-scatter.4.cloned.1.call-start = ((), (), s32[]{:S(2)}) async-start(), calls=%async_computation.2 | async-start | bytes 9437184
  158.1 1.6 copy-start.3
  158.1 1.6 copy-start.11
  162.9 87.8 %copy-start.9 = (f32[64]{0:T(128)S(1)}, f32[64]{0:T(128)}, u32[]{:S(2)}) copy-start(f32[64]{0:T(128)} %param.16) | copy-start | bytes 772
  162.9 87.8 %copy-start.10 = (f32[64]{0:T(128)S(1)}, f32[64]{0:T(128)}, u32[]{:S(2)}) copy-start(f32[64]{0:T(128)} %param.15) | copy-start | bytes 772
  162.9 88.3 %copy-start.6 = (bf16[64,128]{1,0:T(8,128)(2,1)S(1)}, bf16[64,128]{1,0:T(8,128)(2,1)}, u32[]{:S(2)}) copy-start(bf16[64,128]{1,0:T(8,128)(2,1)} %param.17) | copy-start | bytes 49156
  250.2 2.2 copy-start.4
Sparse Core Ops, SparseCore 0:
  23.1 111.8 all-gather.1
  158.3 90.2 reduce-scatter.3
where the time goes:
time: 263 us; the launch traced here: 262 us
  waiting for transfers between devices  196 us (75%)
  local copies, waits for them, and re-layouts  23.7 us (9%)
  matrix products  19 us (7%)
  between operations  13.6 us (5%)
  other arithmetic  9.41 us (4%)
    all_gather x1, waiting for transfers between devices, local(): b_every = lax.all_gather(b_lead, 'row', axis=0, tiled=True)  110 us
    unnamed x3, waiting for transfers between devices  85.7 us
    unnamed x28, local copies, waits for them, and re-layouts  21.3 us
    dot_general x1, matrix products, local(): jnp.einsum('jck,cik->jci', b_every, a_side, preferred_element_type=jnp.fl...  11.4 us
  transfers between devices with their start and end apart: 2, of which 2 were waited for; matrix products, arithmetic and copies ran while one was open for 2% of the time, Pallas kernels for 0%

commit v1 on v0

v1 whole, which is shorter than its diff:
```python
import jax
import jax.numpy as jnp
from jax import lax
from jax.sharding import Mesh
from jax.sharding import PartitionSpec as P

CHIPS = ("xh", "z", "xl", "y")


def normalize(values, gain, bias):
    mean = jnp.mean(values, axis=-1, keepdims=True)
    centered = values - mean
    var = jnp.mean(centered * centered, axis=-1, keepdims=True)
    return centered * lax.rsqrt(var + 1e-05) * gain + bias


def local(pair, in_gain, in_bias, w_proj, w_gate, w_out_gate, out_gain, out_bias, w_out):
    rows, cols, channels = pair.shape
    hidden = w_out.shape[0]
    normed = normalize(pair.astype(jnp.float32), in_gain, in_bias).astype(jnp.bfloat16)
    flat = normed.reshape(-1, channels)
    proj = jnp.dot(flat, w_proj, preferred_element_type=jnp.float32)
    gates = jnp.dot(flat, w_gate, preferred_element_type=jnp.float32)
    both = (jax.nn.sigmoid(gates) * proj).astype(jnp.bfloat16).reshape(rows, cols, 2, hidden)
    lead = jnp.transpose(both, (3, 2, 0, 1))
    chan = lax.all_to_all(lead, CHIPS, 0, 0, tiled=True)
    chan = chan.reshape(2, 4, 2, 4, 2, rows, cols)
    mine = jnp.transpose(chan, (4, 0, 1, 5, 2, 3, 6)).reshape(2, 8 * rows, 8 * cols)
    a_half, b_half = mine[0], mine[1]
    b_other = lax.ppermute(b_half, "core", [(0, 1), (1, 0)])
    core = lax.axis_index("core")
    own = lax.dot_general(a_half, b_half, (((1,), (1,)), ((), ())), preferred_element_type=jnp.float32)
    oth = lax.dot_general(a_half, b_other, (((1,), (1,)), ((), ())), preferred_element_type=jnp.float32)
    own = own.astype(jnp.bfloat16).reshape(2, 4, rows, 2, 4, rows)
    oth = oth.astype(jnp.bfloat16).reshape(2, 4, rows, 2, 4, rows)
    first = jnp.where(core == 0, own, oth)
    second = jnp.where(core == 0, oth, own)
    full = jnp.stack([first, second], axis=5).reshape(2, 4, rows, 2, 4, cols)
    full = jnp.transpose(full, (0, 1, 3, 4, 2, 5)).reshape(64, rows, cols)
    back = lax.all_to_all(full, CHIPS, 0, 0, tiled=True)
    mixed = jnp.transpose(back, (1, 2, 0)).astype(jnp.float32)
    mixed_normed = normalize(mixed, out_gain, out_bias).astype(jnp.bfloat16)
    projected = jnp.dot(mixed_normed.reshape(-1, hidden), w_out, preferred_element_type=jnp.float32)
    out_gates = jax.nn.sigmoid(jnp.dot(flat, w_out_gate, preferred_element_type=jnp.float32))
    update = (out_gates * projected).astype(jnp.bfloat16)
    return update.reshape(rows, cols, channels)


def solution(mesh):
    fine = Mesh(mesh.devices.reshape(2, 4, 2, 2, 4), ("xh", "z", "core", "xl", "y"))
    place = P(("xh", "z", "core"), ("xl", "y"), None)
    return jax.shard_map(
        local,
        mesh=fine,
        in_specs=(place, P(), P(), P(), P(), P(), P(), P(), P()),
        out_specs=place,
        check_vma=False,
    )
```

time: 263 us -> 112 us (0.43)
  waiting for transfers between devices: 196 us -> 16 us
  blocking collectives: 0 us -> 41 us
  between operations: 13.6 us -> 0.27 us
  matrix products: 19 us -> 12.5 us
  starting transfers between devices: 0.26 us -> 6.61 us
  other arithmetic: 9.41 us -> 14.6 us
  local copies, waits for them, and re-layouts: 23.7 us -> 20.7 us
    all_gather x1 -> x0, waiting for transfers between devices: 110 us -> none  [local(): b_every = lax.all_gather(b_lead, 'row', axis=0, tiled=True)]
    unnamed x3 -> x0, waiting for transfers between devices: 85.7 us -> none
    all_to_all x0 -> x1, blocking collectives: none -> 41 us  [local(): chan = lax.all_to_all(lead, CHIPS, 0, 0, tiled=True)]
    unnamed x28 -> x25, local copies, waits for them, and re-layouts: 21.3 us -> 1.87 us
    all_to_all x0 -> x1, waiting for transfers between devices: none -> 15.6 us  [local(): back = lax.all_to_all(full, CHIPS, 0, 0, tiled=True)]
    dot_general x1 -> x2, matrix products: 11.4 us -> 3.52 us  [the longest x1 2.78 us: local(): lax.dot_general(a_half, b_other, (((1,), (1,)), ((), ())), preferred_elem...]
    select_n x0 -> x4, local copies, waits for them, and re-layouts: none -> 7.44 us  [the longest x2 4.55 us: local(): second = jnp.where(core == 0, oth, own)]
    another operation x0 -> x1, other arithmetic: none -> 6.37 us  [local(): full = jnp.stack([first, second], axis=5).reshape(2, 4, rows, 2, 4, cols)]
  transfers between devices with their start and end apart: 2 -> 2, of which waited for: 2 -> 2; matrix products, arithmetic and copies ran while one was open for 2% -> 5% of each run, Pallas kernels for 0% -> 0%
where the time goes in v1:
time: 112 us
  blocking collectives  41 us (37%)
  local copies, waits for them, and re-layouts  20.7 us (18%)
  waiting for transfers between devices  16 us (14%)
  other arithmetic  14.6 us (13%)
  matrix products  12.5 us (11%)
  starting transfers between devices  6.61 us (6%)
    all_to_all x1, blocking collectives, local(): chan = lax.all_to_all(lead, CHIPS, 0, 0, tiled=True)  41 us
    all_to_all x1, waiting for transfers between devices, local(): back = lax.all_to_all(full, CHIPS, 0, 0, tiled=True)  15.6 us
    another operation x1, other arithmetic, local(): full = jnp.stack([first, second], axis=5).reshape(2, 4, rows, 2, 4, cols)  6.37 us
    all_to_all x1, starting transfers between devices, local(): back = lax.all_to_all(full, CHIPS, 0, 0, tiled=True)  6.35 us
    reshape x1, local copies, waits for them, and re-layouts, local(): full = jnp.stack([first, second], axis=5).reshape(2, 4, rows, 2, 4, cols)  4.9 us
    select_n x2, local copies, waits for them, and re-layouts, local(): second = jnp.where(core == 0, oth, own)  4.55 us
    dot_general x1, matrix products, local(): jnp.dot(flat, w_out_gate, preferred_element_type=jnp.float32)  3.19 us
    convert_element_type x1, local copies, waits for them, and re-layouts, local(): (jax.nn.sigmoid(gates) * proj).astype(jnp.bfloat16)  2.9 us
  transfers between devices with their start and end apart: 2, of which 2 were waited for; matrix products, arithmetic and copies ran while one was open for 5% of the time, Pallas kernels for 0%

profile of v1, /device:TPU:0, one launch (start us, length us, event | category | flops | bytes accessed | tf_op | source)
XLA Modules:
  0.0 111.6 jit_solution(14791742767425430787)
XLA Ops:
  0.0 0.0 copy-start
  0.0 0.0 copy-start.1
  0.0 0.0 copy-start.8
  0.0 2.4 %convert_reduce_fusion = f32[64,128]{1,0:T(8,128)S(1)} fusion(bf16[64,128,128]{2,1,0:T(8,128)(2,1)} %param.9), kind=kLoop, calls=%fused_computation.13 | loop fusion | flops 2088960 | bytes 2129920 | tf_op jit(solution)/shard_map/reduce_sum | solution.py:11
  2.4 0.0 copy-done.1
  2.4 2.4 %fusion.10 = f32[64,128]{1,0:T(8,128)S(1)} fusion(bf16[64,128,128]{2,1,0:T(8,128)(2,1)S(1)} %copy-done.1, f32[64,128]{1,0:T(8,128)S(1)} %broadcast_multiply_fusion.1), kind=kLoop, calls=%fused_computation.16 | loop fusion | flops 4186112 | bytes 2162688 | tf_op jit(solution)/shard_map/reduce_sum | solution.py:13
  4.8 0.0 copy-done.8
  4.8 0.0 copy-done.7
  4.8 2.5 %fusion.13 = bf16[64,128,128]{2,1,0:T(8,128)(2,1)S(1)} fusion(bf16[64,128,128]{2,1,0:T(8,128)(2,1)S(1)} %copy-done.1, f32[128]{0:T(128)S(1)} %copy-done.7, f32[128]{0:T(128)S(1)} %copy-done.8, f32[64,128]{1,0:T(8,128)S(1)} %add_rsqrt_fusion.1, f32[64,128]{1,0:T(8,128)S(1)} %broadcast_multiply_fusion.1), kind=kLoop, calls=%fused_computation.19 | loop fusion | flops 6291456 | bytes 4260864 | tf_op jit(solution)/shard_map/convert_element_type | solution.py:20
  7.3 0.0 copy-start.2
  7.4 0.0 copy-done
  7.4 0.0 copy-start.5
  7.4 1.2 %fusion.7 = f32[8192,128]{1,0:T(8,128)S(1)} fusion(bf16[8192,128]{1,0:T(8,128)(2,1)S(1)} %bitcast.49, bf16[128,128]{1,0:T(8,128)(2,1)S(1)} %copy-done), kind=kOutput, calls=%fused_computation.11 | convolution fusion | flops 271581184 | bytes 6324224 | tf_op jit(solution)/shard_map/dot_general | solution.py:23
  8.6 0.0 copy-done.2
  8.7 0.0 copy-done.5
  8.7 2.0 %fusion.4 = bf16[8192,128]{1,0:T(8,128)(2,1)} fusion(f32[8192,128]{1,0:T(8,128)S(1)} %fusion.7, bf16[8192,128]{1,0:T(8,128)(2,1)S(1)} %bitcast.50, bf16[128,128]{1,0:T(8,128)(2,1)S(1)} %copy-done.5), kind=kOutput, calls=%fused_computation.8 | convolution fusion | flops 270532608 | bytes 8421376 | tf_op jit(solution)/shard_map/dot_general | solution.py:22
  10.7 2.9 %copy.16 = bf16[8192,128]{0,1:T(8,128)(2,1)S(1)} copy(bf16[8192,128]{1,0:T(8,128)(2,1)} %fusion.4) | data formatting | bytes 4194304 | tf_op jit(solution)/shard_map/convert_element_type | solution.py:24
  13.6 0.6 copy.22
  14.2 0.2 copy.17
  14.5 41.0 %all_to_all.10 = bf16[64,2,64,128]{3,2,1,0:T(8,128)(2,1)S(1)} all-to-all(bf16[64,2,64,128]{3,2,1,0:T(8,128)(2,1)S(1)} %copy.17), channel_id=1, replica_groups=mesh['xh'=2,'z'=4,'core'=2,'xl'=2,'y'=4] {'xh','z','xl','y'}, dimensions={0} | all-to-all | bytes 4194304 | tf_op jit(solution)/shard_map/all_to_all | solution.py:26
  55.4 0.2 fusion.22
  55.6 0.8 copy.19
  56.4 0.8 squeeze.7
  57.2 0.3 collective-permute-start
  57.5 0.8 copy.18
  58.3 0.8 squeeze.6
  59.1 0.7 convolution_convert_fusion.1
  59.8 0.4 collective-permute-done
  60.2 2.8 %broadcast_select_fusion.1 = (bf16[512,512]{1,0:T(8,128)(2,1)S(1)}, bf16[512,512]{1,0:T(8,128)(2,1)}) fusion(bf16[512,512]{1,0:T(8,128)(2,1)S(1)} %convolution_convert_fusion.1, pred[]{:T(512)S(6)} %eq.4, bf16[512,1024]{1,0:T(8,128)(2,1)S(1)} %squeeze.6, bf16[512,1024]{1,0:T(8,128)(2,1)} %collective-permute-done), kind=kOutput, calls=%fused_computation.34 | convolution fusion | flops 537657344 | bytes 3670017 | tf_op jit(solution)/shard_map/dot_general | solution.py:33
  63.0 0.5 select_n.34
  63.6 2.4 %copy.20 = bf16[2,4,64,2,4,1,64]{6,5,2,4,3,1,0:T(2,128)(2,1)S(1)} copy(bf16[2,4,64,2,4,1,64]{6,4,3,2,1,0,5:T(4,128)(2,1)S(1)} %select_n.34) | data formatting | bytes 1048576 | tf_op jit(solution)/shard_map/jit(_where)/select_n | solution.py:36
  65.9 2.2 %select_n.36 = bf16[2,4,64,2,4,1,64]{6,4,3,2,1,0,5:T(4,128)(2,1)S(1)} reshape(bf16[512,512]{1,0:T(8,128)(2,1)} %get-tuple-element.8) | data formatting | bytes 1048576 | tf_op jit(solution)/shard_map/jit(_where)/select_n | solution.py:37
  68.1 2.4 %copy.21 = bf16[2,4,64,2,4,1,64]{6,5,2,4,3,1,0:T(2,128)(2,1)S(1)} copy(bf16[2,4,64,2,4,1,64]{6,4,3,2,1,0,5:T(4,128)(2,1)S(1)} %select_n.36) | data formatting | bytes 1048576 | tf_op jit(solution)/shard_map/jit(_where)/select_n | solution.py:37
  70.5 6.4 %pad_maximum_fusion = bf16[2,4,64,2,4,2,64]{6,5,2,4,3,1,0:T(2,128)(2,1)} fusion(bf16[2,4,64,2,4,1,64]{6,5,2,4,3,1,0:T(2,128)(2,1)S(1)} %copy.21, bf16[2,4,64,2,4,1,64]{6,5,2,4,3,1,0:T(2,128)(2,1)S(1)} %copy.20), kind=kLoop, calls=%fused_computation.20 | loop fusion | flops 2097152 | bytes 2097152 | tf_op jit(solution)/shard_map/stack | solution.py:38
  76.9 4.9 %reshape.97 = bf16[2,4,64,2,4,128]{5,2,4,3,1,0:T(8,128)(2,1)} reshape(bf16[2,4,64,2,4,2,64]{6,5,2,4,3,1,0:T(2,128)(2,1)} %pad_maximum_fusion) | data formatting | bytes 2097152 | tf_op jit(solution)/shard_map/reshape | solution.py:38
  81.8 6.3 %all-to-all-start.1 = ((bf16[64,64,128]{2,1,0:T(8,128)(2,1)}), bf16[64,64,128]{2,1,0:T(8,128)(2,1)S(1)}, u32[]{:S(2)}, u32[]{:S(2)}) async-start(bf16[64,64,128]{2,1,0:T(8,128)(2,1)} %bitcast.55), calls=%async_computation.1 | async-start | bytes 2097152 | tf_op jit(solution)/shard_map/all_to_all | solution.py:40
  88.1 0.0 copy-done.3
  88.1 0.0 copy-done.11
  88.1 3.2 %fusion.6 = f32[8192,128]{1,0:T(8,128)} fusion(bf16[8192,128]{1,0:T(8,128)(2,1)S(1)} %bitcast.51, bf16[128,128]{1,0:T(8,128)(2,1)S(1)} %copy-done.11), kind=kOutput, calls=%fused_computation.10 | convolution fusion | flops 271581184 | bytes 6324224 | tf_op jit(solution)/shard_map/dot_general | solution.py:44
  91.3 15.6 %all-to-all-done.1 = bf16[64,64,128]{2,1,0:T(8,128)(2,1)S(1)} async-done(((bf16[64,64,128]{2,1,0:T(8,128)(2,1)}), bf16[64,64,128]{2,1,0:T(8,128)(2,1)S(1)}, u32[]{:S(2)}, u32[]{:S(2)}) %all-to-all-start.1) | async-done | bytes 1048608 | tf_op jit(solution)/shard_map/all_to_all | solution.py:40
  106.9 0.2 bitcast_reduce_fusion
  107.1 0.3 fusion.16
  107.4 0.0 copy-done.9
  107.4 0.0 copy-done.10
  107.4 0.5 fusion.19
  107.9 0.0 copy-done.6
  107.9 1.2 %copy-done.4 = f32[8192,128]{1,0:T(8,128)S(1)} copy-done((f32[8192,128]{1,0:T(8,128)S(1)}, f32[8192,128]{1,0:T(8,128)}, u32[]{:S(2)}) %copy-start.4) | copy-done | bytes 4194328
  109.1 2.5 %fusion.5 = bf16[8192,128]{1,0:T(8,128)(2,1)} fusion(f32[8192,128]{1,0:T(8,128)S(1)} %copy-done.4, bf16[64,128]{1,0:T(8,128)(2,1)S(1)} %copy-done.6, bf16[8,8,64,128]{3,2,1,0:T(8,128)(2,1)S(1)} %bitcast.56), kind=kOutput, calls=%fused_computation.9 | convolution fusion | flops 136314880 | bytes 7356416 | tf_op jit(solution)/shard_map/dot_general | solution.py:43
  (11 shorter events, 0.1 us)
Async XLA Ops:
  0.0 7.4 %copy-start = (bf16[128,128]{1,0:T(8,128)(2,1)S(1)}, bf16[128,128]{1,0:T(8,128)(2,1)}, u32[]{:S(2)}) copy-start(bf16[128,128]{1,0:T(8,128)(2,1)} %param.13) | copy-start | bytes 98308
  0.0 2.4 %copy-start.1 = (bf16[64,128,128]{2,1,0:T(8,128)(2,1)S(1)}, bf16[64,128,128]{2,1,0:T(8,128)(2,1)}, u32[]{:S(2)}) copy-start(bf16[64,128,128]{2,1,0:T(8,128)(2,1)} %param.9) | copy-start | bytes 6291460
  0.0 4.8 %copy-start.8 = (f32[128]{0:T(128)S(1)}, f32[128]{0:T(128)}, u32[]{:S(2)}) copy-start(f32[128]{0:T(128)} %param.10) | copy-start | bytes 1540
  0.0 4.8 %copy-start.7 = (f32[128]{0:T(128)S(1)}, f32[128]{0:T(128)}, u32[]{:S(2)}) copy-start(f32[128]{0:T(128)} %param.11) | copy-start | bytes 1540
  7.3 1.3 %copy-start.2 = (bf16[64,128,128]{2,1,0:T(8,128)(2,1)}, bf16[64,128,128]{2,1,0:T(8,128)(2,1)S(1)}, u32[]{:S(2)}) copy-start(bf16[64,128,128]{2,1,0:T(8,128)(2,1)S(1)} %fusion.13) | copy-start | bytes 6291460
  7.4 1.3 %copy-start.5 = (bf16[128,128]{1,0:T(8,128)(2,1)S(1)}, bf16[128,128]{1,0:T(8,128)(2,1)}, u32[]{:S(2)}) copy-start(bf16[128,128]{1,0:T(8,128)(2,1)} %param.12) | copy-start | bytes 98308
  57.2 3.1 %collective-permute-start = (bf16[512,1024]{1,0:T(8,128)(2,1)S(1)}, bf16[512,1024]{1,0:T(8,128)(2,1)}, u32[]{:S(2)}, u32[]{:S(2)}) collective-permute-start(bf16[512,1024]{1,0:T(8,128)(2,1)S(1)} %squeeze.7), channel_id=1, source_target_pairs={{0,8},{8,0},{1,9},{9,1},{2,10},{10,2},{3,11},{11,3},{4,12},{12,4},... | collective-permute-start | bytes 3145736 | tf_op jit(solution)/shard_map/ppermute | solution.py:30
  76.9 11.3 %copy-start.3 = (bf16[64,128,128]{2,1,0:T(8,128)(2,1)S(1)}, bf16[64,128,128]{2,1,0:T(8,128)(2,1)}, u32[]{:S(2)}) copy-start(bf16[64,128,128]{2,1,0:T(8,128)(2,1)} %copy-done.2) | copy-start | bytes 6291460
  76.9 11.3 %copy-start.11 = (bf16[128,128]{1,0:T(8,128)(2,1)S(1)}, bf16[128,128]{1,0:T(8,128)(2,1)}, u32[]{:S(2)}) copy-start(bf16[128,128]{1,0:T(8,128)(2,1)} %param.14) | copy-start | bytes 98308
  81.8 25.1 %all-to-all-start.1 = ((bf16[64,64,128]{2,1,0:T(8,128)(2,1)}), bf16[64,64,128]{2,1,0:T(8,128)(2,1)S(1)}, u32[]{:S(2)}, u32[]{:S(2)}) async-start(bf16[64,64,128]{2,1,0:T(8,128)(2,1)} %bitcast.55), calls=%async_computation.1 | async-start | bytes 2097152 | tf_op jit(solution)/shard_map/all_to_all | solution.py:40
  91.3 16.1 %copy-start.9 = (f32[64]{0:T(128)S(1)}, f32[64]{0:T(128)}, u32[]{:S(2)}) copy-start(f32[64]{0:T(128)} %param.16) | copy-start | bytes 772
  91.3 16.1 %copy-start.10 = (f32[64]{0:T(128)S(1)}, f32[64]{0:T(128)}, u32[]{:S(2)}) copy-start(f32[64]{0:T(128)} %param.15) | copy-start | bytes 772
  91.3 16.6 %copy-start.6 = (bf16[64,128]{1,0:T(8,128)(2,1)S(1)}, bf16[64,128]{1,0:T(8,128)(2,1)}, u32[]{:S(2)}) copy-start(bf16[64,128]{1,0:T(8,128)(2,1)} %param.17) | copy-start | bytes 49156
  106.9 2.2 %copy-start.4 = (f32[8192,128]{1,0:T(8,128)S(1)}, f32[8192,128]{1,0:T(8,128)}, u32[]{:S(2)}) copy-start(f32[8192,128]{1,0:T(8,128)} %fusion.6) | copy-start | bytes 12582916

commit v2 on v1

v2 whole, which is shorter than its diff:
```python
import jax
import jax.numpy as jnp
from jax import lax
from jax.experimental import pallas as pl
from jax.experimental.pallas import tpu as pltpu
from jax.sharding import Mesh
from jax.sharding import PartitionSpec as P

CHIPS = ("xh", "z", "xl", "y")
STEP = 16
EPS = 1e-05
VMEM = 48 << 20
NT = (((1,), (1,)), ((), ()))
TN = (((0,), (0,)), ((), ()))


def sigmoid(x):
    return 0.5 * jnp.tanh(0.5 * x) + 0.5


def normalized(x, gain, bias):
    mean = jnp.mean(x, axis=-1, keepdims=True)
    centered = x - mean
    var = jnp.mean(centered * centered, axis=-1, keepdims=True)
    return (centered * lax.rsqrt(var + EPS) * gain + bias).astype(jnp.bfloat16)


def pre_kernel(pair, gain, bias, w_proj, w_gate, out, weights, held):
    channels = pair.shape[2]
    hidden = channels // 2

    @pl.when(pl.program_id(0) == 0)
    def _():
        weights[:channels] = w_proj[...].T
        weights[channels:] = w_gate[...].T

    for t in range(0, STEP, 2):
        x = pair[t : t + 2].reshape(2 * pair.shape[1], channels).astype(jnp.float32)
        normed = normalized(x, gain[...], bias[...])
        both = lax.dot_general(weights[...], normed, NT, preferred_element_type=jnp.float32)
        y = sigmoid(both[channels:]) * both[:channels]
        held[t] = y[:, : pair.shape[1]]
        held[t + 1] = y[:, pair.shape[1] :]
    for c in range(channels):
        out[c % hidden, c // hidden] = held[:, c, :].astype(jnp.bfloat16)


def pre(pair, gain, bias, w_proj, w_gate):
    rows, cols, channels = pair.shape
    hidden = channels // 2
    whole = lambda *shape: pl.BlockSpec(shape, lambda i: (0,) * len(shape))
    return pl.pallas_call(
        pre_kernel,
        grid=(rows // STEP,),
        in_specs=[
            pl.BlockSpec((STEP, cols, channels), lambda i: (i, 0, 0)),
            whole(1, channels),
            whole(1, channels),
            whole(channels, channels),
            whole(channels, channels),
        ],
        out_specs=pl.BlockSpec((hidden, 2, STEP, cols), lambda i: (0, 0, i, 0)),
        out_shape=jax.ShapeDtypeStruct((hidden, 2, rows, cols), jnp.bfloat16),
        scratch_shapes=[
            pltpu.VMEM((2 * channels, channels), jnp.bfloat16),
            pltpu.VMEM((STEP, channels, cols), jnp.float32),
        ],
        compiler_params=pltpu.CompilerParams(vmem_limit_bytes=VMEM),
        cost_estimate=pl.CostEstimate(flops=1 << 30, bytes_accessed=4 << 20, transcendentals=1 << 20),
        name="pre",
    )(pair, gain, bias, w_proj, w_gate)


def gate_kernel(pair, gain, bias, w_out_gate, out):
    channels = pair.shape[2]
    for t in range(0, STEP, 2):
        x = pair[t : t + 2].reshape(2 * pair.shape[1], channels).astype(jnp.float32)
        normed = normalized(x, gain[...], bias[...])
        gates = jnp.dot(normed, w_out_gate[...], preferred_element_type=jnp.float32)
        out[t : t + 2] = sigmoid(gates).astype(jnp.bfloat16).reshape(2, pair.shape[1], channels)


def gate(pair, gain, bias, w_out_gate):
    rows, cols, channels = pair.shape
    whole = lambda *shape: pl.BlockSpec(shape, lambda i: (0,) * len(shape))
    block = pl.BlockSpec((STEP, cols, channels), lambda i: (i, 0, 0))
    return pl.pallas_call(
        gate_kernel,
        grid=(rows // STEP,),
        in_specs=[block, whole(1, channels), whole(1, channels), whole(channels, channels)],
        out_specs=block,
        out_shape=jax.ShapeDtypeStruct((rows, cols, channels), jnp.bfloat16),
        compiler_params=pltpu.CompilerParams(vmem_limit_bytes=VMEM),
        cost_estimate=pl.CostEstimate(flops=1 << 30, bytes_accessed=16 << 20, transcendentals=1 << 20),
        name="gate",
    )(pair, gain, bias, w_out_gate)


def mid_kernel(core, chan, other, out, a_side, b_side):
    groups, rows, cols = other.shape
    across = 8
    mine = pl.multiple_of(core[0] * rows, rows)
    theirs = pl.multiple_of(rows - core[0] * rows, rows)
    for s in range(groups):
        r, q = s // across, s % across
        here = slice(q * cols, (q + 1) * cols)
        a_side[r * rows : (r + 1) * rows, here] = chan[s, 0]
        b_side[r, pl.ds(mine, rows), here] = chan[s, 1]
        b_side[r, pl.ds(theirs, rows), here] = other[s]
    for g in range(0, across, 2):
        b = b_side[g : g + 2].reshape(2 * cols, across * cols)
        m = lax.dot_general(a_side[...], b, NT, preferred_element_type=jnp.float32).astype(jnp.bfloat16)
        for r in range(groups // across):
            for h in range(2):
                out[r * across + g + h] = m[r * rows : (r + 1) * rows, h * cols : (h + 1) * cols]


def mid(core, chan, other):
    groups, rows, cols = other.shape
    return pl.pallas_call(
        mid_kernel,
        in_specs=[
            pl.BlockSpec(memory_space=pltpu.SMEM),
            pl.BlockSpec(memory_space=pltpu.VMEM),
            pl.BlockSpec(memory_space=pltpu.VMEM),
        ],
        out_specs=pl.BlockSpec(memory_space=pltpu.VMEM),
        out_shape=jax.ShapeDtypeStruct((groups, rows, cols), jnp.bfloat16),
        scratch_shapes=[
            pltpu.VMEM((8 * rows, 8 * cols), jnp.bfloat16),
            pltpu.VMEM((8, 2 * rows, 8 * cols), jnp.bfloat16),
        ],
        compiler_params=pltpu.CompilerParams(vmem_limit_bytes=VMEM),
        cost_estimate=pl.CostEstimate(flops=1 << 30, bytes_accessed=4 << 20, transcendentals=0),
        name="mid",
    )(core, chan, other)


def post_kernel(back, gates, gain, bias, w_out, out, held):
    hidden = back.shape[0]
    m = back[...].astype(jnp.float32)
    mean = jnp.mean(m, axis=0, keepdims=True)
    centered = m - mean
    var = jnp.mean(centered * centered, axis=0, keepdims=True)
    scale = lax.rsqrt(var + EPS)
    for c in range(hidden):
        held[c] = centered[c] * scale[0] * gain[c] + bias[c]
    for t in range(STEP):
        normed = held[:, t, :].astype(jnp.bfloat16)
        projected = lax.dot_general(normed, w_out[...], TN, preferred_element_type=jnp.float32)
        out[t] = (gates[t].astype(jnp.float32) * projected).astype(jnp.bfloat16)


def post(back, gates, gain, bias, w_out):
    hidden, rows, cols = back.shape
    channels = w_out.shape[1]
    block = pl.BlockSpec((STEP, cols, channels), lambda i: (i, 0, 0))
    return pl.pallas_call(
        post_kernel,
        grid=(rows // STEP,),
        in_specs=[
            pl.BlockSpec((hidden, STEP, cols), lambda i: (0, i, 0)),
            block,
            pl.BlockSpec(memory_space=pltpu.SMEM),
            pl.BlockSpec(memory_space=pltpu.SMEM),
            pl.BlockSpec((hidden, channels), lambda i: (0, 0)),
        ],
        out_specs=block,
        out_shape=jax.ShapeDtypeStruct((rows, cols, channels), jnp.bfloat16),
        scratch_shapes=[pltpu.VMEM((hidden, STEP, cols), jnp.float32)],
        compiler_params=pltpu.CompilerParams(vmem_limit_bytes=VMEM),
        cost_estimate=pl.CostEstimate(flops=1 << 28, bytes_accessed=5 << 20, transcendentals=0),
        name="post",
    )(back, gates, gain, bias, w_out)


def local(pair, in_gain, in_bias, w_proj, w_gate, w_out_gate, out_gain, out_bias, w_out):
    gain, bias = in_gain.reshape(1, -1), in_bias.reshape(1, -1)
    lead = pre(pair, gain, bias, w_proj, w_gate)
    gates = gate(pair, gain, bias, w_out_gate)
    chan = lax.all_to_all(lead, CHIPS, 0, 0, tiled=True)
    other = lax.ppermute(chan[:, 1], "core", [(0, 1), (1, 0)])
    core = lax.axis_index("core").astype(jnp.int32).reshape(1)
    back = lax.all_to_all(mid(core, chan, other), CHIPS, 0, 0, tiled=True)
    return post(back, gates, out_gain, out_bias, w_out)


def solution(mesh):
    fine = Mesh(mesh.devices.reshape(2, 4, 2, 2, 4), ("xh", "z", "core", "xl", "y"))
    place = P(("xh", "z", "core"), ("xl", "y"), None)
    return jax.shard_map(
        local,
        mesh=fine,
        in_specs=(place, P(), P(), P(), P(), P(), P(), P(), P()),
        out_specs=place,
        check_vma=False,
    )
```

time: 112 us -> 93.4 us (0.83)
  Pallas kernels: 0 us -> 20.6 us
  other arithmetic: 14.6 us -> 0 us
  matrix products: 12.5 us -> 0 us
  local copies, waits for them, and re-layouts: 20.7 us -> 8.41 us
    pallas_call x0 -> x4, Pallas kernels: none -> 20.6 us  [the longest x1 8.36 us: pre(): pl.pallas_call(pre_kernel, grid=(rows // STEP,), in_specs=[pl.BlockSpec((...]
    dot_general x6 -> x0, matrix products: 12.5 us -> none  [the longest x1 3.19 us: local(): jnp.dot(flat, w_out_gate, preferred_element_type=jnp.float32)]
    select_n x4 -> x0, local copies, waits for them, and re-layouts: 7.44 us -> none  [the longest x2 4.55 us: local(): second = jnp.where(core == 0, oth, own)]
    another operation x1 -> x0, other arithmetic: 6.37 us -> none  [local(): full = jnp.stack([first, second], axis=5).reshape(2, 4, rows, 2, 4, cols)]
    unnamed x25 -> x28, local copies, waits for them, and re-layouts: 1.87 us -> 7.35 us
    reduce_sum x4 -> x0, other arithmetic: 5.23 us -> none  [the longest x2 2.7 us: normalize(): var = jnp.mean(centered * centered, axis=-1, keepdims=True)]
    reshape x1 -> x0, local copies, waits for them, and re-layouts: 4.9 us -> none  [local(): full = jnp.stack([first, second], axis=5).reshape(2, 4, rows, 2, 4, cols)]
    convert_element_type x2 -> x0, other arithmetic: 2.96 us -> none  [the longest x1 2.5 us: local(): normalize(pair.astype(jnp.float32), in_gain, in_bias).astype(jnp.bfloat16)]
  transfers between devices with their start and end apart: 2 -> 2, of which waited for: 2 -> 2; matrix products, arithmetic and copies ran while one was open for 5% -> 0% of each run, Pallas kernels for 0% -> 4%
where the time goes in v2:
time: 93.4 us; the launch traced here: 93 us
  blocking collectives  40.9 us (44%)
  Pallas kernels  20.6 us (22%)
  waiting for transfers between devices  16.7 us (18%)
  local copies, waits for them, and re-layouts  8.41 us (9%)
  starting transfers between devices  6.27 us (7%)
    all_to_all x1, blocking collectives, local(): chan = lax.all_to_all(lead, CHIPS, 0, 0, tiled=True)  40.9 us
    all_to_all x1, waiting for transfers between devices, local(): back = lax.all_to_all(mid(core, chan, other), CHIPS, 0, 0, tiled=True)  13.8 us
    pallas_call x1, Pallas kernels, pre(): pl.pallas_call(pre_kernel, grid=(rows // STEP,), in_specs=[pl.BlockSpec((...  8.36 us
    unnamed x28, local copies, waits for them, and re-layouts  7.35 us
    all_to_all x1, starting transfers between devices, local(): back = lax.all_to_all(mid(core, chan, other), CHIPS, 0, 0, tiled=True)  6.27 us
    pallas_call x1, Pallas kernels, post(): pl.pallas_call(post_kernel, grid=(rows // STEP,), in_specs=[pl.BlockSpec(...  5.65 us
    pallas_call x1, Pallas kernels, gate(): pl.pallas_call(gate_kernel, grid=(rows // STEP,), in_specs=[block, whole(...  3.82 us
    ppermute x1, waiting for transfers between devices, local(): other = lax.ppermute(chan[:, 1], 'core', [(0, 1), (1, 0)])  2.87 us
  transfers between devices with their start and end apart: 2, of which 2 were waited for; matrix products, arithmetic and copies ran while one was open for 0% of the time, Pallas kernels for 4%

profile of v2, /device:TPU:0, one launch (start us, length us, event | category | flops | bytes accessed | tf_op | source)
XLA Modules:
  0.0 93.0 jit_solution(8383031333054506918)
XLA Ops:
  0.0 0.0 copy-start
  0.0 1.6 %copy-done = bf16[64,128,128]{2,1,0:T(8,128)(2,1)S(1)} copy-done((bf16[64,128,128]{2,1,0:T(8,128)(2,1)S(1)}, bf16[64,128,128]{2,1,0:T(8,128)(2,1)}, u32[]{:S(2)}) %copy-start) | copy-done | bytes 2097176
  1.6 0.0 copy-start.4
  1.6 0.8 copy-done.4
  2.4 0.0 copy-start.5
  2.4 0.8 copy-done.5
  3.1 0.0 copy-start.8
  3.1 0.7 copy-done.8
  3.8 0.0 copy-start.10
  3.8 0.7 copy-done.10
  4.4 8.4 %pre.1 = bf16[64,2,64,128]{3,2,1,0:T(8,128)(2,1)S(1)} custom-call(bf16[64,128,128]{2,1,0:T(8,128)(2,1)S(1)} %copy-done, f32[1,128]{1,0:T(1,128)S(1)} %bitcast.7, f32[1,128]{1,0:T(1,128)S(1)} %bitcast.9, bf16[128,128]{1,0:T(8,128)(2,1)S(1)} %copy-done.4, bf16[128,128]{1,0:T(8,128)(2,1)S(1)} %copy-done.5), custom_call_target="tpu_custom_call" | custom-call | flops 1073741824 | bytes 4194304 | tf_op jit(solution)/shard_map/pre/pallas_call | solution.py:52
  12.8 40.9 %all_to_all.10.chan = bf16[64,2,64,128]{3,2,1,0:T(8,128)(2,1)S(1)} all-to-all(bf16[64,2,64,128]{3,2,1,0:T(8,128)(2,1)S(1)} %pre.1), channel_id=1, replica_groups=mesh['xh'=2,'z'=4,'core'=2,'xl'=2,'y'=4] {'xh','z','xl','y'}, dimensions={0} | all-to-all | bytes 4194304 | tf_op jit(solution)/shard_map/all_to_all | solution.py:181
  53.7 1.1 %slice_bitcast_fusion = bf16[64,64,128]{2,1,0:T(8,128)(2,1)} fusion(bf16[64,2,64,128]{3,2,1,0:T(8,128)(2,1)S(1)} %all_to_all.10.chan), kind=kLoop, calls=%fused_computation | loop fusion | bytes 2097152 | tf_op jit(solution)/shard_map/squeeze | solution.py:182
  54.8 0.0 collective-permute-start
  54.8 2.9 %collective-permute-done.other = bf16[64,64,128]{2,1,0:T(8,128)(2,1)S(1)} collective-permute-done((bf16[64,64,128]{2,1,0:T(8,128)(2,1)}, bf16[64,64,128]{2,1,0:T(8,128)(2,1)S(1)}, u32[]{:S(2)}, u32[]{:S(2)}) %collective-permute-start) | collective-permute-done | bytes 1048608 | tf_op jit(solution)/shard_map/ppermute | solution.py:182
  57.7 0.0 copy-start.6
  57.7 0.0 copy-start.9
  57.7 0.0 copy-start.11
  57.7 2.8 %mid.1 = bf16[64,64,128]{2,1,0:T(8,128)(2,1)} custom-call(s32[1]{0:T(128)} %bitcast.core, bf16[64,2,64,128]{3,2,1,0:T(8,128)(2,1)S(1)} %all_to_all.10.chan, bf16[64,64,128]{2,1,0:T(8,128)(2,1)S(1)} %collective-permute-done.other), custom_call_target="tpu_custom_call" | custom-call | flops 1073741824 | bytes 4194304 | tf_op jit(solution)/shard_map/mid/pallas_call | solution.py:120
  60.4 0.0 copy-start.1
  60.4 6.3 %all-to-all-start.1 = ((bf16[64,64,128]{2,1,0:T(8,128)(2,1)}), bf16[64,64,128]{2,1,0:T(8,128)(2,1)S(1)}, u32[]{:S(2)}, u32[]{:S(2)}) async-start(bf16[64,64,128]{2,1,0:T(8,128)(2,1)} %mid.1), calls=%async_computation.1 | async-start | bytes 2097152 | tf_op jit(solution)/shard_map/all_to_all | solution.py:184
  66.7 0.0 copy-done.6
  66.7 0.0 copy-done.9
  66.7 0.0 copy-done.11
  66.7 0.0 copy-done.1
  66.8 0.0 copy-start.7
  66.8 0.0 copy-start.12
  66.8 0.0 copy-start.13
  66.8 3.8 %gate.1.gates = bf16[64,128,128]{2,1,0:T(8,128)(2,1)S(1)} custom-call(bf16[64,128,128]{2,1,0:T(8,128)(2,1)S(1)} %copy-done.1, f32[1,128]{1,0:T(1,128)S(1)} %bitcast.8, f32[1,128]{1,0:T(1,128)S(1)} %bitcast.10, bf16[128,128]{1,0:T(8,128)(2,1)S(1)} %copy-done.6), custom_call_target="tpu_custom_call" | custom-call | flops 1073741824 | bytes 16777216 | tf_op jit(solution)/shard_map/gate/pallas_call | solution.py:87
  70.6 0.0 copy-start.2
  70.6 1.3 %copy-done.2 = bf16[64,128,128]{2,1,0:T(8,128)(2,1)} copy-done((bf16[64,128,128]{2,1,0:T(8,128)(2,1)}, bf16[64,128,128]{2,1,0:T(8,128)(2,1)S(1)}, u32[]{:S(2)}) %copy-start.2) | copy-done | bytes 2097176
  71.9 13.8 %all-to-all-done.1.back = bf16[64,64,128]{2,1,0:T(8,128)(2,1)S(1)} async-done(((bf16[64,64,128]{2,1,0:T(8,128)(2,1)}), bf16[64,64,128]{2,1,0:T(8,128)(2,1)S(1)}, u32[]{:S(2)}, u32[]{:S(2)}) %all-to-all-start.1) | async-done | bytes 1048608 | tf_op jit(solution)/shard_map/all_to_all | solution.py:184
  85.7 0.0 copy-done.7
  85.7 0.0 copy-done.12
  85.7 0.0 copy-done.13
  85.7 0.0 copy-start.3
  85.8 1.6 %copy-done.3 = bf16[64,128,128]{2,1,0:T(8,128)(2,1)S(1)} copy-done((bf16[64,128,128]{2,1,0:T(8,128)(2,1)S(1)}, bf16[64,128,128]{2,1,0:T(8,128)(2,1)}, u32[]{:S(2)}) %copy-start.3) | copy-done | bytes 2097176
  87.3 5.6 %post.1 = bf16[64,128,128]{2,1,0:T(8,128)(2,1)} custom-call(bf16[64,64,128]{2,1,0:T(8,128)(2,1)S(1)} %all-to-all-done.1.back, bf16[64,128,128]{2,1,0:T(8,128)(2,1)S(1)} %copy-done.3, f32[64]{0:T(128)S(1)} %copy-done.12, f32[64]{0:T(128)S(1)} %copy-done.13, bf16[64,128]{1,0:T(8,128)(2,1)S(1)} %copy-done.7), custom_call_target="tpu_custom_call" | custom-call | flops 268435456 | bytes 5242880 | tf_op jit(solution)/shard_map/post/pallas_call | solution.py:158
Async XLA Ops:
  0.0 1.6 %copy-start = (bf16[64,128,128]{2,1,0:T(8,128)(2,1)S(1)}, bf16[64,128,128]{2,1,0:T(8,128)(2,1)}, u32[]{:S(2)}) copy-start(bf16[64,128,128]{2,1,0:T(8,128)(2,1)} %pair.3) | copy-start | bytes 6291460
  1.6 0.8 copy-start.4
  2.4 0.8 copy-start.5
  3.1 0.7 copy-start.8
  3.8 0.7 copy-start.10
  54.8 2.9 %collective-permute-start = (bf16[64,64,128]{2,1,0:T(8,128)(2,1)}, bf16[64,64,128]{2,1,0:T(8,128)(2,1)S(1)}, u32[]{:S(2)}, u32[]{:S(2)}) collective-permute-start(bf16[64,64,128]{2,1,0:T(8,128)(2,1)} %slice_bitcast_fusion), channel_id=1, source_target_pairs={{0,8},{8,0},{1,9},{9,1},{2,10},{10,2},{3,11},{11,3},{4,12},{12,4},... | collective-permute-start | bytes 3145736 | tf_op jit(solution)/shard_map/ppermute | solution.py:182
  57.7 9.1 %copy-start.6 = (bf16[128,128]{1,0:T(8,128)(2,1)S(1)}, bf16[128,128]{1,0:T(8,128)(2,1)}, u32[]{:S(2)}) copy-start(bf16[128,128]{1,0:T(8,128)(2,1)} %w_out_gate.1) | copy-start | bytes 98308
  57.7 9.1 %copy-start.9 = (f32[128]{0:T(128)S(1)}, f32[128]{0:T(128)}, u32[]{:S(2)}) copy-start(f32[128]{0:T(128)} %param.10) | copy-start | bytes 1540
  57.7 9.1 %copy-start.11 = (f32[128]{0:T(128)S(1)}, f32[128]{0:T(128)}, u32[]{:S(2)}) copy-start(f32[128]{0:T(128)} %param.11) | copy-start | bytes 1540
  60.4 6.3 %copy-start.1 = (bf16[64,128,128]{2,1,0:T(8,128)(2,1)S(1)}, bf16[64,128,128]{2,1,0:T(8,128)(2,1)}, u32[]{:S(2)}) copy-start(bf16[64,128,128]{2,1,0:T(8,128)(2,1)} %pair.3) | copy-start | bytes 6291460
  60.4 25.3 %all-to-all-start.1 = ((bf16[64,64,128]{2,1,0:T(8,128)(2,1)}), bf16[64,64,128]{2,1,0:T(8,128)(2,1)S(1)}, u32[]{:S(2)}, u32[]{:S(2)}) async-start(bf16[64,64,128]{2,1,0:T(8,128)(2,1)} %mid.1), calls=%async_computation.1 | async-start | bytes 2097152 | tf_op jit(solution)/shard_map/all_to_all | solution.py:184
  66.8 19.0 %copy-start.7 = (bf16[64,128]{1,0:T(8,128)(2,1)S(1)}, bf16[64,128]{1,0:T(8,128)(2,1)}, u32[]{:S(2)}) copy-start(bf16[64,128]{1,0:T(8,128)(2,1)} %w_out.1) | copy-start | bytes 49156
  66.8 19.0 %copy-start.12 = (f32[64]{0:T(128)S(1)}, f32[64]{0:T(128)}, u32[]{:S(2)}) copy-start(f32[64]{0:T(128)} %gain.1) | copy-start | bytes 772
  66.8 19.0 %copy-start.13 = (f32[64]{0:T(128)S(1)}, f32[64]{0:T(128)}, u32[]{:S(2)}) copy-start(f32[64]{0:T(128)} %bias.1) | copy-start | bytes 772
  70.6 1.3 %copy-start.2 = (bf16[64,128,128]{2,1,0:T(8,128)(2,1)}, bf16[64,128,128]{2,1,0:T(8,128)(2,1)S(1)}, u32[]{:S(2)}) copy-start(bf16[64,128,128]{2,1,0:T(8,128)(2,1)S(1)} %gate.1.gates) | copy-start | bytes 6291460
  85.7 1.6 %copy-start.3 = (bf16[64,128,128]{2,1,0:T(8,128)(2,1)S(1)}, bf16[64,128,128]{2,1,0:T(8,128)(2,1)}, u32[]{:S(2)}) copy-start(bf16[64,128,128]{2,1,0:T(8,128)(2,1)} %copy-done.2) | copy-start | bytes 6291460

commit v3 on v2

v3 whole, which is shorter than its diff:
```python
import jax
import jax.numpy as jnp
from jax import lax
from jax.experimental import pallas as pl
from jax.experimental.pallas import tpu as pltpu
from jax.sharding import Mesh
from jax.sharding import PartitionSpec as P

CHIPS = ("xh", "z", "xl", "y")
STEP = 16
EPS = 1e-05
FEW = 24 << 20
VMEM = 48 << 20
NEARLY = 60 << 20
MOST = 58 << 20
NT = (((1,), (1,)), ((), ()))
TN = (((0,), (0,)), ((), ()))


def sigmoid(x):
    return 0.5 * jnp.tanh(0.5 * x) + 0.5


def normalized(x, gain, bias):
    share = 1.0 / x.shape[-1]
    centered = x - jnp.sum(x, axis=-1, keepdims=True) * share
    var = jnp.sum(centered * centered, axis=-1, keepdims=True) * share
    return (centered * lax.rsqrt(var + EPS) * gain + bias).astype(jnp.bfloat16)


def copies(pairs, sems):
    return [pltpu.make_async_copy(src, dst, sems.at[n]) for n, (src, dst) in enumerate(pairs)]


def chunks(source, target, sems):
    rows = target.shape[0]
    spans = [slice(s, s + STEP) for s in range(0, rows, STEP)]
    return copies([(source.at[span], target.at[span]) for span in spans], sems)


def pre_kernel(pair, gain, bias, w_proj, w_gate, out, held, made, affine, loaded, weights, gains, biases, sems, held_sems, out_sems):
    rows, cols, channels = held.shape
    hidden = channels // 2
    small = copies(
        [(gain, affine.at[0:1]), (bias, affine.at[1:2]), (w_proj, loaded.at[0]), (w_gate, loaded.at[1])], sems
    )
    large = chunks(pair, held, held_sems)
    for copy in small + large:
        copy.start()
    for copy in small:
        copy.wait()
    weights[:channels] = loaded[0].T
    weights[channels:] = loaded[1].T
    gains[...] = jnp.broadcast_to(affine[0:1], (cols, channels)).T
    biases[...] = jnp.broadcast_to(affine[1:2], (cols, channels)).T

    def products(first):
        x = held[first : first + 2].reshape(2 * cols, channels).T.astype(jnp.float32)
        centered = x - jnp.sum(x, axis=0, keepdims=True) * (1.0 / channels)
        var = jnp.sum(centered * centered, axis=0, keepdims=True) * (1.0 / channels)
        x = centered * lax.rsqrt(var + EPS)
        normed = [x[:, h * cols : (h + 1) * cols] * gains[...] + biases[...] for h in range(2)]
        normed = jnp.concatenate(normed, axis=1).astype(jnp.bfloat16)
        both = jnp.dot(weights[...], normed, preferred_element_type=jnp.float32)
        return (sigmoid(both[channels:]) * both[:channels]).astype(jnp.bfloat16)

    spans = [slice(s, s + STEP) for s in range(0, rows, STEP)]
    writes = copies([(made.at[:, :, span], out.at[:, :, span]) for span in spans], out_sems)
    for s in range(0, rows, STEP):
        large[s // STEP].wait()
        y = [products(s + t) for t in range(0, STEP, 2)]
        for c in range(0, channels, 16):
            lead = jnp.stack([v[c : c + 16, h * cols : (h + 1) * cols] for v in y for h in range(2)], axis=0)
            made[c % hidden : c % hidden + 16, c // hidden, s : s + STEP] = jnp.swapaxes(lead, 0, 1)
        writes[s // STEP].start()
    for copy in writes:
        copy.wait()


def pre(pair, gain, bias, w_proj, w_gate):
    rows, cols, channels = pair.shape
    hidden = channels // 2
    return pl.pallas_call(
        pre_kernel,
        in_specs=[pl.BlockSpec(memory_space=pl.ANY)] * 5,
        out_specs=pl.BlockSpec(memory_space=pl.ANY),
        out_shape=jax.ShapeDtypeStruct((hidden, 2, rows, cols), jnp.bfloat16),
        scratch_shapes=[
            pltpu.VMEM((rows, cols, channels), jnp.bfloat16),
            pltpu.VMEM((hidden, 2, rows, cols), jnp.bfloat16),
            pltpu.VMEM((2, channels), jnp.float32),
            pltpu.VMEM((2, channels, channels), jnp.bfloat16),
            pltpu.VMEM((2 * channels, channels), jnp.bfloat16),
            pltpu.VMEM((channels, cols), jnp.float32),
            pltpu.VMEM((channels, cols), jnp.float32),
            pltpu.SemaphoreType.DMA((4,)),
            pltpu.SemaphoreType.DMA((rows // STEP,)),
            pltpu.SemaphoreType.DMA((rows // STEP,)),
        ],
        compiler_params=pltpu.CompilerParams(vmem_limit_bytes=MOST),
        cost_estimate=pl.CostEstimate(flops=1 << 30, bytes_accessed=4 << 20, transcendentals=1 << 20),
        name="pre",
    )(pair, gain, bias, w_proj, w_gate)


def gate_kernel(pair, gain, bias, w_out_gate, out, held, affine, loaded, sems, held_sems):
    rows, cols, channels = held.shape
    small = copies([(gain, affine.at[0:1]), (bias, affine.at[1:2]), (w_out_gate, loaded)], sems)
    large = chunks(pair, held, held_sems)
    for copy in small + large:
        copy.start()
    for copy in small:
        copy.wait()
    for s in range(0, rows, STEP):
        large[s // STEP].wait()
        for t in range(s, s + STEP, 2):
            x = held[t : t + 2].reshape(2 * cols, channels).astype(jnp.float32)
            normed = normalized(x, affine[0:1], affine[1:2])
            gates = jnp.dot(normed, loaded[...], preferred_element_type=jnp.float32)
            out[t : t + 2] = sigmoid(gates).astype(jnp.bfloat16).reshape(2, cols, channels)


def gate(pair, gain, bias, w_out_gate):
    rows, cols, channels = pair.shape
    return pl.pallas_call(
        gate_kernel,
        in_specs=[pl.BlockSpec(memory_space=pl.ANY)] * 4,
        out_specs=pl.BlockSpec(memory_space=pltpu.VMEM),
        out_shape=jax.ShapeDtypeStruct((rows, cols, channels), jnp.bfloat16),
        scratch_shapes=[
            pltpu.VMEM((rows, cols, channels), jnp.bfloat16),
            pltpu.VMEM((2, channels), jnp.float32),
            pltpu.VMEM((channels, channels), jnp.bfloat16),
            pltpu.SemaphoreType.DMA((3,)),
            pltpu.SemaphoreType.DMA((rows // STEP,)),
        ],
        compiler_params=pltpu.CompilerParams(vmem_limit_bytes=NEARLY),
        cost_estimate=pl.CostEstimate(flops=1 << 30, bytes_accessed=16 << 20, transcendentals=1 << 20),
        name="gate",
    )(pair, gain, bias, w_out_gate)


def mid_kernel(core, chan, other, out, a_side, b_side):
    groups, rows, cols = other.shape
    across = 8
    mine = pl.multiple_of(core[0] * rows, rows)
    theirs = pl.multiple_of(rows - core[0] * rows, rows)
    for s in range(groups):
        r, q = s // across, s % across
        here = slice(q * cols, (q + 1) * cols)
        a_side[r * rows : (r + 1) * rows, here] = chan[s, 0]
        b_side[r, pl.ds(mine, rows), here] = chan[s, 1]
        b_side[r, pl.ds(theirs, rows), here] = other[s]
    for g in range(0, across, 2):
        b = b_side[g : g + 2].reshape(2 * cols, across * cols)
        m = lax.dot_general(a_side[...], b, NT, preferred_element_type=jnp.float32).astype(jnp.bfloat16)
        for r in range(groups // across):
            for h in range(2):
                out[r * across + g + h] = m[r * rows : (r + 1) * rows, h * cols : (h + 1) * cols]


def mid(core, chan, other):
    groups, rows, cols = other.shape
    return pl.pallas_call(
        mid_kernel,
        in_specs=[
            pl.BlockSpec(memory_space=pltpu.SMEM),
            pl.BlockSpec(memory_space=pltpu.VMEM),
            pl.BlockSpec(memory_space=pltpu.VMEM),
        ],
        out_specs=pl.BlockSpec(memory_space=pltpu.VMEM),
        out_shape=jax.ShapeDtypeStruct((groups, rows, cols), jnp.bfloat16),
        scratch_shapes=[
            pltpu.VMEM((8 * rows, 8 * cols), jnp.bfloat16),
            pltpu.VMEM((8, 2 * rows, 8 * cols), jnp.bfloat16),
        ],
        compiler_params=pltpu.CompilerParams(vmem_limit_bytes=VMEM),
        cost_estimate=pl.CostEstimate(flops=1 << 30, bytes_accessed=4 << 20, transcendentals=0),
        name="mid",
    )(core, chan, other)


def post_kernel(back, gates, gain, bias, w_out, out, made, loaded, wide, sem, out_sems):
    hidden, rows, cols = back.shape
    channels = loaded.shape[1]
    weight = pltpu.make_async_copy(w_out, loaded, sem)
    weight.start()
    wide[...] = jnp.zeros_like(wide)
    weight.wait()
    wide[:hidden, :channels] = loaded[...]
    wide[hidden:, channels:] = loaded[...]
    writes = chunks(made, out, out_sems)
    for s in range(0, rows, STEP):
        m = back[:, s : s + STEP, :].astype(jnp.float32)
        centered = m - jnp.sum(m, axis=0) * (1.0 / hidden)
        scale = lax.rsqrt(jnp.sum(centered * centered, axis=0) * (1.0 / hidden) + EPS)
        turned = []
        for c in range(0, hidden, 8):
            lead = jnp.stack([centered[c + d] * scale * gain[c + d] + bias[c + d] for d in range(8)], axis=0)
            turned.append(jnp.swapaxes(lead, 0, 1))
        normed = jnp.concatenate(turned, axis=1).astype(jnp.bfloat16)
        for t in range(0, STEP, 2):
            two = normed[t : t + 2].reshape(2 * hidden, cols)
            projected = lax.dot_general(two, wide[...], TN, preferred_element_type=jnp.float32)
            for h in range(2):
                mine = projected[:, h * channels : (h + 1) * channels]
                made[s + t + h] = (gates[s + t + h].astype(jnp.float32) * mine).astype(jnp.bfloat16)
        writes[s // STEP].start()
    for copy in writes:
        copy.wait()


def post(back, gates, gain, bias, w_out):
    hidden, rows, cols = back.shape
    channels = w_out.shape[1]
    whole = pl.BlockSpec(memory_space=pl.ANY)
    scalars = pl.BlockSpec(memory_space=pltpu.SMEM)
    return pl.pallas_call(
        post_kernel,
        in_specs=[pl.BlockSpec(memory_space=pltpu.VMEM)] * 2 + [scalars, scalars, whole],
        out_specs=whole,
        out_shape=jax.ShapeDtypeStruct((rows, cols, channels), jnp.bfloat16),
        scratch_shapes=[
            pltpu.VMEM((rows, cols, channels), jnp.bfloat16),
            pltpu.VMEM((hidden, channels), jnp.bfloat16),
            pltpu.VMEM((2 * hidden, 2 * channels), jnp.bfloat16),
            pltpu.SemaphoreType.DMA,
            pltpu.SemaphoreType.DMA((rows // STEP,)),
        ],
        compiler_params=pltpu.CompilerParams(vmem_limit_bytes=FEW),
        cost_estimate=pl.CostEstimate(flops=1 << 28, bytes_accessed=5 << 20, transcendentals=0),
        name="post",
    )(back, gates, gain, bias, w_out)


def local(pair, in_gain, in_bias, w_proj, w_gate, w_out_gate, out_gain, out_bias, w_out):
    gain, bias = in_gain.reshape(1, -1), in_bias.reshape(1, -1)
    lead = pre(pair, gain, bias, w_proj, w_gate)
    gates = gate(pair, gain, bias, w_out_gate)
    chan = lax.all_to_all(lead, CHIPS, 0, 0, tiled=True)
    chan, gates = lax.optimization_barrier((chan, gates))
    other = lax.ppermute(chan[:, 1], "core", [(0, 1), (1, 0)])
    core = lax.axis_index("core").astype(jnp.int32).reshape(1)
    back = lax.all_to_all(mid(core, chan, other), CHIPS, 0, 0, tiled=True)
    return post(back, gates, out_gain, out_bias, w_out)


def solution(mesh):
    fine = Mesh(mesh.devices.reshape(2, 4, 2, 2, 4), ("xh", "z", "core", "xl", "y"))
    place = P(("xh", "z", "core"), ("xl", "y"), None)
    return jax.shard_map(
        local,
        mesh=fine,
        in_specs=(place, P(), P(), P(), P(), P(), P(), P(), P()),
        out_specs=place,
        check_vma=False,
    )
```

time: 93.4 us -> 81.4 us (0.87)
  blocking collectives: 40.9 us -> 25 us
  waiting for transfers between devices: 16.7 us -> 26.1 us
  local copies, waits for them, and re-layouts: 8.41 us -> 1.08 us
  starting transfers between devices: 6.27 us -> 11.5 us
  Pallas kernels: 20.6 us -> 17.4 us
    all_to_all x1, blocking collectives: 40.9 us -> 25 us  [local(): back = lax.all_to_all(mid(core, chan, other), CHIPS, 0, 0, tiled=True)]
    all_to_all x1, waiting for transfers between devices: 13.8 us -> 23.2 us  [local(): chan = lax.all_to_all(lead, CHIPS, 0, 0, tiled=True)]
    unnamed x28 -> x8, local copies, waits for them, and re-layouts: 7.35 us -> 0.02 us
    all_to_all x1, starting transfers between devices: 6.27 us -> 11.5 us  [local(): chan = lax.all_to_all(lead, CHIPS, 0, 0, tiled=True)]
    pallas_call x3, Pallas kernels: 17.8 us -> 15.6 us  [the longest x1 6.46 us: gate(): pl.pallas_call(gate_kernel, in_specs=[pl.BlockSpec(memory_space=pl.ANY)]...]
    pallas_call x1, Pallas kernels: 2.76 us -> 1.78 us  [mid(): pl.pallas_call(mid_kernel, in_specs=[pl.BlockSpec(memory_space=pltpu.SMEM...]
  transfers between devices with their start and end apart: 2 -> 2, of which waited for: 2 -> 2; matrix products, arithmetic and copies ran while one was open for 0% -> 0% of each run, Pallas kernels for 4% -> 8%
where the time goes in v3:
time: 81.4 us; the launch traced here: 81.1 us
  waiting for transfers between devices  26.1 us (32%)
  blocking collectives  25 us (31%)
  Pallas kernels  17.4 us (21%)
  starting transfers between devices  11.5 us (14%)
  local copies, waits for them, and re-layouts  1.08 us (1%)
    all_to_all x1, blocking collectives, local(): back = lax.all_to_all(mid(core, chan, other), CHIPS, 0, 0, tiled=True)  25 us
    all_to_all x1, waiting for transfers between devices, local(): chan = lax.all_to_all(lead, CHIPS, 0, 0, tiled=True)  23.2 us
    all_to_all x1, starting transfers between devices, local(): chan = lax.all_to_all(lead, CHIPS, 0, 0, tiled=True)  11.5 us
    pallas_call x1, Pallas kernels, gate(): pl.pallas_call(gate_kernel, in_specs=[pl.BlockSpec(memory_space=pl.ANY)]...  6.46 us
    pallas_call x1, Pallas kernels, pre(): pl.pallas_call(pre_kernel, in_specs=[pl.BlockSpec(memory_space=pl.ANY)] *...  5.69 us
    pallas_call x1, Pallas kernels, post(): pl.pallas_call(post_kernel, in_specs=[pl.BlockSpec(memory_space=pltpu.VME...  3.44 us
    ppermute x1, waiting for transfers between devices, local(): other = lax.ppermute(chan[:, 1], 'core', [(0, 1), (1, 0)])  2.87 us
    pallas_call x1, Pallas kernels, mid(): pl.pallas_call(mid_kernel, in_specs=[pl.BlockSpec(memory_space=pltpu.SMEM...  1.78 us
  transfers between devices with their start and end apart: 2, of which 2 were waited for; matrix products, arithmetic and copies ran while one was open for 0% of the time, Pallas kernels for 8%

profile of v3, /device:TPU:0, one launch (start us, length us, event | category | flops | bytes accessed | tf_op | source)
XLA Modules:
  0.0 81.1 jit_solution(12479996728162814218)
XLA Ops:
  0.0 5.7 %pre.1 = bf16[64,2,64,128]{3,2,1,0:T(8,128)(2,1)} custom-call(bf16[64,128,128]{2,1,0:T(8,128)(2,1)} %pair.3, f32[1,128]{1,0:T(1,128)} %bitcast.5, f32[1,128]{1,0:T(1,128)} %bitcast.7, bf16[128,128]{1,0:T(8,128)(2,1)} %w_proj.1, bf16[128,128]{1,0:T(8,128)(2,1)} %w_gate.1), custom_call_target="tpu_custom_call" | custom-call | flops 1073741824 | bytes 4194304 | tf_op jit(solution)/shard_map/pre/pallas_call | solution.py:83
  5.7 11.5 %all-to-all-start = ((bf16[64,2,64,128]{3,2,1,0:T(8,128)(2,1)}), bf16[64,2,64,128]{3,2,1,0:T(8,128)(2,1)S(1)}, u32[]{:S(2)}, u32[]{:S(2)}) async-start(bf16[64,2,64,128]{3,2,1,0:T(8,128)(2,1)} %pre.1), calls=%async_computation | async-start | bytes 4194304 | tf_op jit(solution)/shard_map/all_to_all | solution.py:240
  17.2 6.5 %gate.1.gates = bf16[64,128,128]{2,1,0:T(8,128)(2,1)} custom-call(bf16[64,128,128]{2,1,0:T(8,128)(2,1)} %pair.3, f32[1,128]{1,0:T(1,128)} %bitcast.6, f32[1,128]{1,0:T(1,128)} %bitcast.8, bf16[128,128]{1,0:T(8,128)(2,1)} %w_out_gate.1), custom_call_target="tpu_custom_call" | custom-call | flops 1073741824 | bytes 16777216 | tf_op jit(solution)/shard_map/gate/pallas_call | solution.py:125
  23.7 23.2 %all-to-all-done.chan = bf16[64,2,64,128]{3,2,1,0:T(8,128)(2,1)S(1)} async-done(((bf16[64,2,64,128]{3,2,1,0:T(8,128)(2,1)}), bf16[64,2,64,128]{3,2,1,0:T(8,128)(2,1)S(1)}, u32[]{:S(2)}, u32[]{:S(2)}) %all-to-all-start) | async-done | bytes 2097184 | tf_op jit(solution)/shard_map/all_to_all | solution.py:240
  46.9 1.1 %slice_bitcast_fusion = bf16[64,64,128]{2,1,0:T(8,128)(2,1)} fusion(bf16[64,2,64,128]{3,2,1,0:T(8,128)(2,1)S(1)} %all-to-all-done.chan), kind=kLoop, calls=%fused_computation | loop fusion | bytes 2097152 | tf_op jit(solution)/shard_map/squeeze | solution.py:242
  47.9 0.0 collective-permute-start
  47.9 2.9 %collective-permute-done.other = bf16[64,64,128]{2,1,0:T(8,128)(2,1)S(1)} collective-permute-done((bf16[64,64,128]{2,1,0:T(8,128)(2,1)}, bf16[64,64,128]{2,1,0:T(8,128)(2,1)S(1)}, u32[]{:S(2)}, u32[]{:S(2)}) %collective-permute-start) | collective-permute-done | bytes 1048608 | tf_op jit(solution)/shard_map/ppermute | solution.py:242
  50.8 0.0 copy-start.1
  50.8 0.0 copy-start.2
  50.8 0.0 copy-start.3
  50.8 1.8 %mid.1 = bf16[64,64,128]{2,1,0:T(8,128)(2,1)S(1)} custom-call(s32[1]{0:T(128)} %bitcast.core, bf16[64,2,64,128]{3,2,1,0:T(8,128)(2,1)S(1)} %all-to-all-done.chan, bf16[64,64,128]{2,1,0:T(8,128)(2,1)S(1)} %collective-permute-done.other), custom_call_target="tpu_custom_call" | custom-call | flops 1073741824 | bytes 4194304 | tf_op jit(solution)/shard_map/mid/pallas_call | solution.py:164
  52.6 0.0 copy-start
  52.6 25.0 %all_to_all.10.back = bf16[64,64,128]{2,1,0:T(8,128)(2,1)S(1)} all-to-all(bf16[64,64,128]{2,1,0:T(8,128)(2,1)S(1)} %mid.1), channel_id=1, replica_groups=mesh['xh'=2,'z'=4,'core'=2,'xl'=2,'y'=4] {'xh','z','xl','y'}, dimensions={0} | all-to-all | bytes 2097152 | tf_op jit(solution)/shard_map/all_to_all | solution.py:244
  77.6 0.0 copy-done.1
  77.6 0.0 copy-done.2
  77.6 0.0 copy-done.3
  77.7 0.0 copy-done
  77.7 3.4 %post.1 = bf16[64,128,128]{2,1,0:T(8,128)(2,1)} custom-call(bf16[64,64,128]{2,1,0:T(8,128)(2,1)S(1)} %all_to_all.10.back, bf16[64,128,128]{2,1,0:T(8,128)(2,1)S(1)} %copy-done, f32[64]{0:T(128)S(1)} %copy-done.2, f32[64]{0:T(128)S(1)} %copy-done.3, bf16[64,128]{1,0:T(8,128)(2,1)S(1)} %copy-done.1), custom_call_target="tpu_custom_call" | custom-call | flops 268435456 | bytes 5242880 | tf_op jit(solution)/shard_map/post/pallas_call | solution.py:218
Async XLA Ops:
  5.7 41.2 %all-to-all-start = ((bf16[64,2,64,128]{3,2,1,0:T(8,128)(2,1)}), bf16[64,2,64,128]{3,2,1,0:T(8,128)(2,1)S(1)}, u32[]{:S(2)}, u32[]{:S(2)}) async-start(bf16[64,2,64,128]{3,2,1,0:T(8,128)(2,1)} %pre.1), calls=%async_computation | async-start | bytes 4194304 | tf_op jit(solution)/shard_map/all_to_all | solution.py:240
  47.9 2.9 %collective-permute-start = (bf16[64,64,128]{2,1,0:T(8,128)(2,1)}, bf16[64,64,128]{2,1,0:T(8,128)(2,1)S(1)}, u32[]{:S(2)}, u32[]{:S(2)}) collective-permute-start(bf16[64,64,128]{2,1,0:T(8,128)(2,1)} %slice_bitcast_fusion), channel_id=1, source_target_pairs={{0,8},{8,0},{1,9},{9,1},{2,10},{10,2},{3,11},{11,3},{4,12},{12,4},... | collective-permute-start | bytes 3145736 | tf_op jit(solution)/shard_map/ppermute | solution.py:242
  50.8 26.8 %copy-start.1 = (bf16[64,128]{1,0:T(8,128)(2,1)S(1)}, bf16[64,128]{1,0:T(8,128)(2,1)}, u32[]{:S(2)}) copy-start(bf16[64,128]{1,0:T(8,128)(2,1)} %w_out.1) | copy-start | bytes 49156
  50.8 26.8 %copy-start.2 = (f32[64]{0:T(128)S(1)}, f32[64]{0:T(128)}, u32[]{:S(2)}) copy-start(f32[64]{0:T(128)} %gain.1) | copy-start | bytes 772
  50.8 26.8 %copy-start.3 = (f32[64]{0:T(128)S(1)}, f32[64]{0:T(128)}, u32[]{:S(2)}) copy-start(f32[64]{0:T(128)} %bias.1) | copy-start | bytes 772
  52.6 25.1 %copy-start = (bf16[64,128,128]{2,1,0:T(8,128)(2,1)S(1)}, bf16[64,128,128]{2,1,0:T(8,128)(2,1)}, u32[]{:S(2)}) copy-start(bf16[64,128,128]{2,1,0:T(8,128)(2,1)} %gate.1.gates) | copy-start | bytes 6291460

commit v4 on v3

--- a/solution.py
+++ b/solution.py
@@ -6,7 +6,8 @@
 from jax.sharding import Mesh
 from jax.sharding import PartitionSpec as P
 
-CHIPS = ("xh", "z", "xl", "y")
+CHIPS = ("xh", "z", "y", "xl")
+PLACES = [(xh * 4 + z, xl * 4 + y) for xh in range(2) for z in range(4) for y in range(4) for xl in range(2)]
 STEP = 16
 EPS = 1e-05
 FEW = 24 << 20
@@ -49,8 +50,9 @@
         copy.start()
     for copy in small:
         copy.wait()
-    weights[:channels] = loaded[0].T
-    weights[channels:] = loaded[1].T
+    for n in range(2):
+        half = loaded[n].astype(jnp.float32).T * 0.5
+        weights[n * channels : (n + 1) * channels] = half.astype(jnp.bfloat16)
     gains[...] = jnp.broadcast_to(affine[0:1], (cols, channels)).T
     biases[...] = jnp.broadcast_to(affine[1:2], (cols, channels)).T
 
@@ -62,7 +64,7 @@
         normed = [x[:, h * cols : (h + 1) * cols] * gains[...] + biases[...] for h in range(2)]
         normed = jnp.concatenate(normed, axis=1).astype(jnp.bfloat16)
         both = jnp.dot(weights[...], normed, preferred_element_type=jnp.float32)
-        return (sigmoid(both[channels:]) * both[:channels]).astype(jnp.bfloat16)
+        return (jnp.tanh(both[channels:]) * both[:channels] + both[:channels]).astype(jnp.bfloat16)
 
     spans = [slice(s, s + STEP) for s in range(0, rows, STEP)]
     writes = copies([(made.at[:, :, span], out.at[:, :, span]) for span in spans], out_sems)
@@ -145,8 +147,7 @@
     across = 8
     mine = pl.multiple_of(core[0] * rows, rows)
     theirs = pl.multiple_of(rows - core[0] * rows, rows)
-    for s in range(groups):
-        r, q = s // across, s % across
+    for s, (r, q) in enumerate(PLACES):
         here = slice(q * cols, (q + 1) * cols)
         a_side[r * rows : (r + 1) * rows, here] = chan[s, 0]
         b_side[r, pl.ds(mine, rows), here] = chan[s, 1]
@@ -156,7 +157,7 @@
         m = lax.dot_general(a_side[...], b, NT, preferred_element_type=jnp.float32).astype(jnp.bfloat16)
         for r in range(groups // across):
             for h in range(2):
-                out[r * across + g + h] = m[r * rows : (r + 1) * rows, h * cols : (h + 1) * cols]
+                out[PLACES.index((r, g + h))] = m[r * rows : (r + 1) * rows, h * cols : (h + 1) * cols]
 
 
 def mid(core, chan, other):
@@ -195,10 +196,10 @@
         centered = m - jnp.sum(m, axis=0) * (1.0 / hidden)
         scale = lax.rsqrt(jnp.sum(centered * centered, axis=0) * (1.0 / hidden) + EPS)
         turned = []
-        for c in range(0, hidden, 8):
-            lead = jnp.stack([centered[c + d] * scale * gain[c + d] + bias[c + d] for d in range(8)], axis=0)
-            turned.append(jnp.swapaxes(lead, 0, 1))
-        normed = jnp.concatenate(turned, axis=1).astype(jnp.bfloat16)
+        for c in range(0, hidden, 16):
+            lead = jnp.stack([centered[c + d] * scale * gain[c + d] + bias[c + d] for d in range(16)], axis=0)
+            turned.append(jnp.swapaxes(lead.astype(jnp.bfloat16), 0, 1))
+        normed = jnp.concatenate(turned, axis=1)
         for t in range(0, STEP, 2):
             two = normed[t : t + 2].reshape(2 * hidden, cols)
             projected = lax.dot_general(two, wide[...], TN, preferred_element_type=jnp.float32)

time: 81.4 us -> 79.2 us (0.973)
  waiting for transfers between devices: 26.1 us -> 24.8 us
    all_to_all x1, waiting for transfers between devices: 23.2 us -> 21.9 us  [local(): chan = lax.all_to_all(lead, CHIPS, 0, 0, tiled=True)]
where the time goes in v4:
time: 79.2 us; the launch traced here: 78.9 us
  waiting for transfers between devices  24.8 us (31%)
  blocking collectives  24.3 us (31%)
  Pallas kernels  17.2 us (22%)
  starting transfers between devices  11.5 us (15%)
  local copies, waits for them, and re-layouts  1.08 us (1%)
    all_to_all x1, blocking collectives, local(): back = lax.all_to_all(mid(core, chan, other), CHIPS, 0, 0, tiled=True)  24.3 us
    all_to_all x1, waiting for transfers between devices, local(): chan = lax.all_to_all(lead, CHIPS, 0, 0, tiled=True)  21.9 us
    all_to_all x1, starting transfers between devices, local(): chan = lax.all_to_all(lead, CHIPS, 0, 0, tiled=True)  11.5 us
    pallas_call x1, Pallas kernels, gate(): pl.pallas_call(gate_kernel, in_specs=[pl.BlockSpec(memory_space=pl.ANY)]...  6.45 us
    pallas_call x1, Pallas kernels, pre(): pl.pallas_call(pre_kernel, in_specs=[pl.BlockSpec(memory_space=pl.ANY)] *...  5.64 us
    pallas_call x1, Pallas kernels, post(): pl.pallas_call(post_kernel, in_specs=[pl.BlockSpec(memory_space=pltpu.VME...  3.3 us
    ppermute x1, waiting for transfers between devices, local(): other = lax.ppermute(chan[:, 1], 'core', [(0, 1), (1, 0)])  2.87 us
    pallas_call x1, Pallas kernels, mid(): pl.pallas_call(mid_kernel, in_specs=[pl.BlockSpec(memory_space=pltpu.SMEM...  1.78 us
  transfers between devices with their start and end apart: 2, of which 2 were waited for; matrix products, arithmetic and copies ran while one was open for 0% of the time, Pallas kernels for 8%

profile of v4, /device:TPU:0, one launch (start us, length us, event | category | flops | bytes accessed | tf_op | source)
XLA Modules:
  0.0 78.9 jit_solution(15984517684043758166)
XLA Ops:
  0.0 5.6 %pre.1 = bf16[64,2,64,128]{3,2,1,0:T(8,128)(2,1)} custom-call(bf16[64,128,128]{2,1,0:T(8,128)(2,1)} %pair.3, f32[1,128]{1,0:T(1,128)} %bitcast.5, f32[1,128]{1,0:T(1,128)} %bitcast.7, bf16[128,128]{1,0:T(8,128)(2,1)} %w_proj.1, bf16[128,128]{1,0:T(8,128)(2,1)} %w_gate.1), custom_call_target="tpu_custom_call" | custom-call | flops 1073741824 | bytes 4194304 | tf_op jit(solution)/shard_map/pre/pallas_call | solution.py:85
  5.6 11.5 %all-to-all-start = ((bf16[64,2,64,128]{3,2,1,0:T(8,128)(2,1)}), bf16[64,2,64,128]{3,2,1,0:T(8,128)(2,1)S(1)}, u32[]{:S(2)}, u32[]{:S(2)}) async-start(bf16[64,2,64,128]{3,2,1,0:T(8,128)(2,1)} %pre.1), calls=%async_computation | async-start | bytes 4194304 | tf_op jit(solution)/shard_map/all_to_all | solution.py:241
  17.2 6.5 %gate.1.gates = bf16[64,128,128]{2,1,0:T(8,128)(2,1)} custom-call(bf16[64,128,128]{2,1,0:T(8,128)(2,1)} %pair.3, f32[1,128]{1,0:T(1,128)} %bitcast.6, f32[1,128]{1,0:T(1,128)} %bitcast.8, bf16[128,128]{1,0:T(8,128)(2,1)} %w_out_gate.1), custom_call_target="tpu_custom_call" | custom-call | flops 1073741824 | bytes 16777216 | tf_op jit(solution)/shard_map/gate/pallas_call | solution.py:127
  23.6 21.9 %all-to-all-done.chan = bf16[64,2,64,128]{3,2,1,0:T(8,128)(2,1)S(1)} async-done(((bf16[64,2,64,128]{3,2,1,0:T(8,128)(2,1)}), bf16[64,2,64,128]{3,2,1,0:T(8,128)(2,1)S(1)}, u32[]{:S(2)}, u32[]{:S(2)}) %all-to-all-start) | async-done | bytes 2097184 | tf_op jit(solution)/shard_map/all_to_all | solution.py:241
  45.5 1.1 %slice_bitcast_fusion = bf16[64,64,128]{2,1,0:T(8,128)(2,1)} fusion(bf16[64,2,64,128]{3,2,1,0:T(8,128)(2,1)S(1)} %all-to-all-done.chan), kind=kLoop, calls=%fused_computation | loop fusion | bytes 2097152 | tf_op jit(solution)/shard_map/squeeze | solution.py:243
  46.6 0.0 collective-permute-start
  46.6 2.9 %collective-permute-done.other = bf16[64,64,128]{2,1,0:T(8,128)(2,1)S(1)} collective-permute-done((bf16[64,64,128]{2,1,0:T(8,128)(2,1)}, bf16[64,64,128]{2,1,0:T(8,128)(2,1)S(1)}, u32[]{:S(2)}, u32[]{:S(2)}) %collective-permute-start) | collective-permute-done | bytes 1048608 | tf_op jit(solution)/shard_map/ppermute | solution.py:243
  49.5 0.0 copy-start.1
  49.5 0.0 copy-start.2
  49.5 0.0 copy-start.3
  49.5 1.8 %mid.1 = bf16[64,64,128]{2,1,0:T(8,128)(2,1)S(1)} custom-call(s32[1]{0:T(128)} %bitcast.core, bf16[64,2,64,128]{3,2,1,0:T(8,128)(2,1)S(1)} %all-to-all-done.chan, bf16[64,64,128]{2,1,0:T(8,128)(2,1)S(1)} %collective-permute-done.other), custom_call_target="tpu_custom_call" | custom-call | flops 1073741824 | bytes 4194304 | tf_op jit(solution)/shard_map/mid/pallas_call | solution.py:165
  51.3 0.0 copy-start
  51.3 24.3 %all_to_all.10.back = bf16[64,64,128]{2,1,0:T(8,128)(2,1)S(1)} all-to-all(bf16[64,64,128]{2,1,0:T(8,128)(2,1)S(1)} %mid.1), channel_id=1, replica_groups=mesh['xh'=2,'z'=4,'core'=2,'xl'=2,'y'=4] {'xh','z','y','xl'}, dimensions={0} | all-to-all | bytes 2097152 | tf_op jit(solution)/shard_map/all_to_all | solution.py:245
  75.6 0.0 copy-done.1
  75.6 0.0 copy-done.2
  75.6 0.0 copy-done.3
  75.6 0.0 copy-done
  75.6 3.3 %post.1 = bf16[64,128,128]{2,1,0:T(8,128)(2,1)} custom-call(bf16[64,64,128]{2,1,0:T(8,128)(2,1)S(1)} %all_to_all.10.back, bf16[64,128,128]{2,1,0:T(8,128)(2,1)S(1)} %copy-done, f32[64]{0:T(128)S(1)} %copy-done.2, f32[64]{0:T(128)S(1)} %copy-done.3, bf16[64,128]{1,0:T(8,128)(2,1)S(1)} %copy-done.1), custom_call_target="tpu_custom_call" | custom-call | flops 268435456 | bytes 5242880 | tf_op jit(solution)/shard_map/post/pallas_call | solution.py:219
Async XLA Ops:
  5.6 39.9 %all-to-all-start = ((bf16[64,2,64,128]{3,2,1,0:T(8,128)(2,1)}), bf16[64,2,64,128]{3,2,1,0:T(8,128)(2,1)S(1)}, u32[]{:S(2)}, u32[]{:S(2)}) async-start(bf16[64,2,64,128]{3,2,1,0:T(8,128)(2,1)} %pre.1), calls=%async_computation | async-start | bytes 4194304 | tf_op jit(solution)/shard_map/all_to_all | solution.py:241
  46.6 2.9 %collective-permute-start = (bf16[64,64,128]{2,1,0:T(8,128)(2,1)}, bf16[64,64,128]{2,1,0:T(8,128)(2,1)S(1)}, u32[]{:S(2)}, u32[]{:S(2)}) collective-permute-start(bf16[64,64,128]{2,1,0:T(8,128)(2,1)} %slice_bitcast_fusion), channel_id=1, source_target_pairs={{0,8},{8,0},{1,9},{9,1},{2,10},{10,2},{3,11},{11,3},{4,12},{12,4},... | collective-permute-start | bytes 3145736 | tf_op jit(solution)/shard_map/ppermute | solution.py:243
  49.5 26.1 %copy-start.1 = (bf16[64,128]{1,0:T(8,128)(2,1)S(1)}, bf16[64,128]{1,0:T(8,128)(2,1)}, u32[]{:S(2)}) copy-start(bf16[64,128]{1,0:T(8,128)(2,1)} %w_out.1) | copy-start | bytes 49156
  49.5 26.1 %copy-start.2 = (f32[64]{0:T(128)S(1)}, f32[64]{0:T(128)}, u32[]{:S(2)}) copy-start(f32[64]{0:T(128)} %gain.1) | copy-start | bytes 772
  49.5 26.1 %copy-start.3 = (f32[64]{0:T(128)S(1)}, f32[64]{0:T(128)}, u32[]{:S(2)}) copy-start(f32[64]{0:T(128)} %bias.1) | copy-start | bytes 772
  51.3 24.4 %copy-start = (bf16[64,128,128]{2,1,0:T(8,128)(2,1)S(1)}, bf16[64,128,128]{2,1,0:T(8,128)(2,1)}, u32[]{:S(2)}) copy-start(bf16[64,128,128]{2,1,0:T(8,128)(2,1)} %gate.1.gates) | copy-start | bytes 6291460

commit v5 on v4

--- a/solution.py
+++ b/solution.py
@@ -142,43 +142,81 @@
     )(pair, gain, bias, w_out_gate)
 
 
-def mid_kernel(core, chan, other, out, a_side, b_side):
+def spread(a_side, b_side, side, put):
+    cols = 128
+    for n in range(0, b_side.shape[0], 2 * cols):
+        b = b_side[n : n + 2 * cols]
+        m = lax.dot_general(a_side[...], b, NT, preferred_element_type=jnp.float32)
+        for h in range(2):
+            block = m[:, h * cols : (h + 1) * cols]
+            turned = pltpu.roll(block, cols // 2, 1)
+            low = jnp.full(block.shape, side, jnp.int32) == 0
+            g = (n + h * cols) // (cols // 2)
+            put(g, jnp.where(low, block, turned))
+            put(g + 1, jnp.where(low, turned, block))
+
+
+def own_kernel(core, chan, a_side, out, b_side):
+    rows, cols = chan.shape[2:]
+    for s, (r, q) in enumerate(PLACES):
+        here = slice(r * rows, (r + 1) * rows), slice(q * cols, (q + 1) * cols)
+        a_side[here] = chan[s, 0]
+        b_side[here] = chan[s, 1]
+
+    def put(g, m):
+        for r in range(8):
+            out[PLACES.index((r, g))] = m[r * rows : (r + 1) * rows].astype(jnp.bfloat16)
+
+    spread(a_side, b_side, core[0], put)
+
+
+def own(core, chan):
+    groups, _, rows, cols = chan.shape
+    vmem = pl.BlockSpec(memory_space=pltpu.VMEM)
+    return pl.pallas_call(
+        own_kernel,
+        in_specs=[pl.BlockSpec(memory_space=pltpu.SMEM), vmem],
+        out_specs=[vmem, vmem],
+        out_shape=[
+            jax.ShapeDtypeStruct((8 * rows, 8 * cols), jnp.bfloat16),
+            jax.ShapeDtypeStruct((groups, rows, cols), jnp.bfloat16),
+        ],
+        scratch_shapes=[pltpu.VMEM((8 * rows, 8 * cols), jnp.bfloat16)],
+        compiler_params=pltpu.CompilerParams(vmem_limit_bytes=VMEM),
+        cost_estimate=pl.CostEstimate(flops=1 << 29, bytes_accessed=4 << 20, transcendentals=0),
+        name="own",
+    )(core, chan)
+
+
+def mid_kernel(core, a_side, mine, other, out, b_side):
+    rows, cols = other.shape[1:]
+    side = 1 - core[0]
+    for s, (r, q) in enumerate(PLACES):
+        b_side[r * rows : (r + 1) * rows, q * cols : (q + 1) * cols] = other[s]
+    lanes = lax.broadcasted_iota(jnp.int32, (rows, cols), 1) // (cols // 2) == side
+
+    def put(g, m):
+        for r in range(8):
+            s = PLACES.index((r, g))
+            part = jnp.where(lanes, m[r * rows : (r + 1) * rows], mine[s].astype(jnp.float32))
+            out[s] = part.astype(jnp.bfloat16)
+
+    spread(a_side, b_side, side, put)
+
+
+def mid(core, a_side, mine, other):
     groups, rows, cols = other.shape
-    across = 8
-    mine = pl.multiple_of(core[0] * rows, rows)
-    theirs = pl.multiple_of(rows - core[0] * rows, rows)
-    for s, (r, q) in enumerate(PLACES):
-        here = slice(q * cols, (q + 1) * cols)
-        a_side[r * rows : (r + 1) * rows, here] = chan[s, 0]
-        b_side[r, pl.ds(mine, rows), here] = chan[s, 1]
-        b_side[r, pl.ds(theirs, rows), here] = other[s]
-    for g in range(0, across, 2):
-        b = b_side[g : g + 2].reshape(2 * cols, across * cols)
-        m = lax.dot_general(a_side[...], b, NT, preferred_element_type=jnp.float32).astype(jnp.bfloat16)
-        for r in range(groups // across):
-            for h in range(2):
-                out[PLACES.index((r, g + h))] = m[r * rows : (r + 1) * rows, h * cols : (h + 1) * cols]
-
-
-def mid(core, chan, other):
-    groups, rows, cols = other.shape
+    vmem = pl.BlockSpec(memory_space=pltpu.VMEM)
     return pl.pallas_call(
         mid_kernel,
-        in_specs=[
-            pl.BlockSpec(memory_space=pltpu.SMEM),
-            pl.BlockSpec(memory_space=pltpu.VMEM),
-            pl.BlockSpec(memory_space=pltpu.VMEM),
-        ],
-        out_specs=pl.BlockSpec(memory_space=pltpu.VMEM),
+        in_specs=[pl.BlockSpec(memory_space=pltpu.SMEM), vmem, vmem, vmem],
+        out_specs=vmem,
         out_shape=jax.ShapeDtypeStruct((groups, rows, cols), jnp.bfloat16),
-        scratch_shapes=[
-            pltpu.VMEM((8 * rows, 8 * cols), jnp.bfloat16),
-            pltpu.VMEM((8, 2 * rows, 8 * cols), jnp.bfloat16),
-        ],
+        scratch_shapes=[pltpu.VMEM((8 * rows, 8 * cols), jnp.bfloat16)],
         compiler_params=pltpu.CompilerParams(vmem_limit_bytes=VMEM),
-        cost_estimate=pl.CostEstimate(flops=1 << 30, bytes_accessed=4 << 20, transcendentals=0),
+        cost_estimate=pl.CostEstimate(flops=1 << 29, bytes_accessed=4 << 20, transcendentals=0),
         name="mid",
-    )(core, chan, other)
+    )(core, a_side, mine, other)
 
 
 def post_kernel(back, gates, gain, bias, w_out, out, made, loaded, wide, sem, out_sems):
@@ -186,12 +224,11 @@
     channels = loaded.shape[1]
     weight = pltpu.make_async_copy(w_out, loaded, sem)
     weight.start()
-    wide[...] = jnp.zeros_like(wide)
-    weight.wait()
-    wide[:hidden, :channels] = loaded[...]
-    wide[hidden:, channels:] = loaded[...]
-    writes = chunks(made, out, out_sems)
-    for s in range(0, rows, STEP):
+    ends = [*range(STEP, rows, STEP), rows - STEP // 2, rows]
+    spans = [slice(first, end) for first, end in zip([0] + ends, ends)]
+    writes = copies([(made.at[span], out.at[span]) for span in spans], out_sems)
+
+    def mixed(s):
         m = back[:, s : s + STEP, :].astype(jnp.float32)
         centered = m - jnp.sum(m, axis=0) * (1.0 / hidden)
         scale = lax.rsqrt(jnp.sum(centered * centered, axis=0) * (1.0 / hidden) + EPS)
@@ -199,14 +236,24 @@
         for c in range(0, hidden, 16):
             lead = jnp.stack([centered[c + d] * scale * gain[c + d] + bias[c + d] for d in range(16)], axis=0)
             turned.append(jnp.swapaxes(lead.astype(jnp.bfloat16), 0, 1))
-        normed = jnp.concatenate(turned, axis=1)
+        return jnp.concatenate(turned, axis=1)
+
+    normed = mixed(0)
+    wide[...] = jnp.zeros_like(wide)
+    weight.wait()
+    wide[:hidden, :channels] = loaded[...]
+    wide[hidden:, channels:] = loaded[...]
+    for s in range(0, rows, STEP):
+        later = mixed(s + STEP) if s + STEP < rows else None
         for t in range(0, STEP, 2):
             two = normed[t : t + 2].reshape(2 * hidden, cols)
             projected = lax.dot_general(two, wide[...], TN, preferred_element_type=jnp.float32)
             for h in range(2):
                 mine = projected[:, h * channels : (h + 1) * channels]
                 made[s + t + h] = (gates[s + t + h].astype(jnp.float32) * mine).astype(jnp.bfloat16)
-        writes[s // STEP].start()
+            if s + t + 2 in ends:
+                writes[ends.index(s + t + 2)].start()
+        normed = later
     for copy in writes:
         copy.wait()
 
@@ -226,7 +273,7 @@
             pltpu.VMEM((hidden, channels), jnp.bfloat16),
             pltpu.VMEM((2 * hidden, 2 * channels), jnp.bfloat16),
             pltpu.SemaphoreType.DMA,
-            pltpu.SemaphoreType.DMA((rows // STEP,)),
+            pltpu.SemaphoreType.DMA((rows // STEP + 1,)),
         ],
         compiler_params=pltpu.CompilerParams(vmem_limit_bytes=FEW),
         cost_estimate=pl.CostEstimate(flops=1 << 28, bytes_accessed=5 << 20, transcendentals=0),
@@ -242,7 +289,7 @@
     chan, gates = lax.optimization_barrier((chan, gates))
     other = lax.ppermute(chan[:, 1], "core", [(0, 1), (1, 0)])
     core = lax.axis_index("core").astype(jnp.int32).reshape(1)
-    back = lax.all_to_all(mid(core, chan, other), CHIPS, 0, 0, tiled=True)
+    back = lax.all_to_all(mid(core, *own(core, chan), other), CHIPS, 0, 0, tiled=True)
     return post(back, gates, out_gain, out_bias, w_out)
 
 

time: 79.2 us -> 78.4 us (0.990)
  waiting for transfers between devices: 24.8 us -> 23.9 us
    ppermute x1, waiting for transfers between devices: 2.87 us -> 1.96 us  [local(): other = lax.ppermute(chan[:, 1], 'core', [(0, 1), (1, 0)])]
    pallas_call x0 -> x1, Pallas kernels: none -> 0.9 us  [own(): pl.pallas_call(own_kernel, in_specs=[pl.BlockSpec(memory_space=pltpu.SMEM...]
  transfers between devices with their start and end apart: 2 -> 2, of which waited for: 2 -> 2; matrix products, arithmetic and copies ran while one was open for 0% -> 0% of each run, Pallas kernels for 8% -> 9%
where the time goes in v5:
time: 78.4 us; the launch traced here: 78.1 us
  blocking collectives  24.3 us (31%)
  waiting for transfers between devices  23.9 us (30%)
  Pallas kernels  17.3 us (22%)
  starting transfers between devices  11.5 us (15%)
  local copies, waits for them, and re-layouts  1.08 us (1%)
    all_to_all x1, blocking collectives, local(): lax.all_to_all(mid(core, *own(core, chan), other), CHIPS, 0, 0, tiled=True)  24.3 us
    all_to_all x1, waiting for transfers between devices, local(): chan = lax.all_to_all(lead, CHIPS, 0, 0, tiled=True)  21.9 us
    all_to_all x1, starting transfers between devices, local(): chan = lax.all_to_all(lead, CHIPS, 0, 0, tiled=True)  11.5 us
    pallas_call x1, Pallas kernels, gate(): pl.pallas_call(gate_kernel, in_specs=[pl.BlockSpec(memory_space=pl.ANY)]...  6.45 us
    pallas_call x1, Pallas kernels, pre(): pl.pallas_call(pre_kernel, in_specs=[pl.BlockSpec(memory_space=pl.ANY)] *...  5.64 us
    pallas_call x1, Pallas kernels, post(): pl.pallas_call(post_kernel, in_specs=[pl.BlockSpec(memory_space=pltpu.VME...  3.28 us
    ppermute x1, waiting for transfers between devices, local(): other = lax.ppermute(chan[:, 1], 'core', [(0, 1), (1, 0)])  1.96 us
  transfers between devices with their start and end apart: 2, of which 2 were waited for; matrix products, arithmetic and copies ran while one was open for 0% of the time, Pallas kernels for 9%

profile of v5, /device:TPU:0, one launch (start us, length us, event | category | flops | bytes accessed | tf_op | source)
XLA Modules:
  0.0 78.1 jit_solution(13007529810806372035)
XLA Ops:
  0.0 5.6 %pre.1 = bf16[64,2,64,128]{3,2,1,0:T(8,128)(2,1)} custom-call(bf16[64,128,128]{2,1,0:T(8,128)(2,1)} %pair.3, f32[1,128]{1,0:T(1,128)} %bitcast.5, f32[1,128]{1,0:T(1,128)} %bitcast.7, bf16[128,128]{1,0:T(8,128)(2,1)} %w_proj.1, bf16[128,128]{1,0:T(8,128)(2,1)} %w_gate.1), custom_call_target="tpu_custom_call" | custom-call | flops 1073741824 | bytes 4194304 | tf_op jit(solution)/shard_map/pre/pallas_call | solution.py:85
  5.6 11.5 %all-to-all-start = ((bf16[64,2,64,128]{3,2,1,0:T(8,128)(2,1)}), bf16[64,2,64,128]{3,2,1,0:T(8,128)(2,1)S(1)}, u32[]{:S(2)}, u32[]{:S(2)}) async-start(bf16[64,2,64,128]{3,2,1,0:T(8,128)(2,1)} %pre.1), calls=%async_computation | async-start | bytes 4194304 | tf_op jit(solution)/shard_map/all_to_all | solution.py:288
  17.2 6.5 %gate.1.gates = bf16[64,128,128]{2,1,0:T(8,128)(2,1)} custom-call(bf16[64,128,128]{2,1,0:T(8,128)(2,1)} %pair.3, f32[1,128]{1,0:T(1,128)} %bitcast.6, f32[1,128]{1,0:T(1,128)} %bitcast.8, bf16[128,128]{1,0:T(8,128)(2,1)} %w_out_gate.1), custom_call_target="tpu_custom_call" | custom-call | flops 1073741824 | bytes 16777216 | tf_op jit(solution)/shard_map/gate/pallas_call | solution.py:127
  23.6 21.9 %all-to-all-done.chan = bf16[64,2,64,128]{3,2,1,0:T(8,128)(2,1)S(1)} async-done(((bf16[64,2,64,128]{3,2,1,0:T(8,128)(2,1)}), bf16[64,2,64,128]{3,2,1,0:T(8,128)(2,1)S(1)}, u32[]{:S(2)}, u32[]{:S(2)}) %all-to-all-start) | async-done | bytes 2097184 | tf_op jit(solution)/shard_map/all_to_all | solution.py:288
  45.5 1.1 %slice_bitcast_fusion = bf16[64,64,128]{2,1,0:T(8,128)(2,1)} fusion(bf16[64,2,64,128]{3,2,1,0:T(8,128)(2,1)S(1)} %all-to-all-done.chan), kind=kLoop, calls=%fused_computation | loop fusion | bytes 2097152 | tf_op jit(solution)/shard_map/squeeze | solution.py:290
  46.6 0.0 collective-permute-start
  46.6 0.9 %own.1 = (bf16[512,1024]{1,0:T(8,128)(2,1)S(1)}, bf16[64,64,128]{2,1,0:T(8,128)(2,1)S(1)}) custom-call(s32[1]{0:T(128)} %bitcast.core, bf16[64,2,64,128]{3,2,1,0:T(8,128)(2,1)S(1)} %all-to-all-done.chan), custom_call_target="tpu_custom_call" | custom-call | flops 536870912 | bytes 4194304 | tf_op jit(solution)/shard_map/own/pallas_call | solution.py:176
  47.5 2.0 %collective-permute-done.other = bf16[64,64,128]{2,1,0:T(8,128)(2,1)S(1)} collective-permute-done((bf16[64,64,128]{2,1,0:T(8,128)(2,1)}, bf16[64,64,128]{2,1,0:T(8,128)(2,1)S(1)}, u32[]{:S(2)}, u32[]{:S(2)}) %collective-permute-start) | collective-permute-done | bytes 1048608 | tf_op jit(solution)/shard_map/ppermute | solution.py:290
  49.5 0.0 copy-start.1
  49.5 0.0 copy-start.2
  49.5 0.0 copy-start.3
  49.5 1.0 %mid.1 = bf16[64,64,128]{2,1,0:T(8,128)(2,1)S(1)} custom-call(s32[1]{0:T(128)} %bitcast.core, bf16[512,1024]{1,0:T(8,128)(2,1)S(1)} %get-tuple-element.10.a_side, bf16[64,64,128]{2,1,0:T(8,128)(2,1)S(1)} %get-tuple-element.11.mine, bf16[64,64,128]{2,1,0:T(8,128)(2,1)S(1)} %collective-permute-done.other), custom_call_target="tpu_custom_call" | custom-call | flops 536870912 | bytes 4194304 | tf_op jit(solution)/shard_map/mid/pallas_call | solution.py:210
  50.5 0.0 copy-start
  50.5 24.3 %all_to_all.10.back = bf16[64,64,128]{2,1,0:T(8,128)(2,1)S(1)} all-to-all(bf16[64,64,128]{2,1,0:T(8,128)(2,1)S(1)} %mid.1), channel_id=1, replica_groups=mesh['xh'=2,'z'=4,'core'=2,'xl'=2,'y'=4] {'xh','z','y','xl'}, dimensions={0} | all-to-all | bytes 2097152 | tf_op jit(solution)/shard_map/all_to_all | solution.py:292
  74.8 0.0 copy-done.1
  74.9 0.0 copy-done.2
  74.9 0.0 copy-done.3
  74.9 0.0 copy-done
  74.9 3.3 %post.1 = bf16[64,128,128]{2,1,0:T(8,128)(2,1)} custom-call(bf16[64,64,128]{2,1,0:T(8,128)(2,1)S(1)} %all_to_all.10.back, bf16[64,128,128]{2,1,0:T(8,128)(2,1)S(1)} %copy-done, f32[64]{0:T(128)S(1)} %copy-done.2, f32[64]{0:T(128)S(1)} %copy-done.3, bf16[64,128]{1,0:T(8,128)(2,1)S(1)} %copy-done.1), custom_call_target="tpu_custom_call" | custom-call | flops 268435456 | bytes 5242880 | tf_op jit(solution)/shard_map/post/pallas_call | solution.py:266
Async XLA Ops:
  5.6 39.9 %all-to-all-start = ((bf16[64,2,64,128]{3,2,1,0:T(8,128)(2,1)}), bf16[64,2,64,128]{3,2,1,0:T(8,128)(2,1)S(1)}, u32[]{:S(2)}, u32[]{:S(2)}) async-start(bf16[64,2,64,128]{3,2,1,0:T(8,128)(2,1)} %pre.1), calls=%async_computation | async-start | bytes 4194304 | tf_op jit(solution)/shard_map/all_to_all | solution.py:288
  46.6 2.9 %collective-permute-start = (bf16[64,64,128]{2,1,0:T(8,128)(2,1)}, bf16[64,64,128]{2,1,0:T(8,128)(2,1)S(1)}, u32[]{:S(2)}, u32[]{:S(2)}) collective-permute-start(bf16[64,64,128]{2,1,0:T(8,128)(2,1)} %slice_bitcast_fusion), channel_id=1, source_target_pairs={{0,8},{8,0},{1,9},{9,1},{2,10},{10,2},{3,11},{11,3},{4,12},{12,4},... | collective-permute-start | bytes 3145736 | tf_op jit(solution)/shard_map/ppermute | solution.py:290
  49.5 25.4 %copy-start.1 = (bf16[64,128]{1,0:T(8,128)(2,1)S(1)}, bf16[64,128]{1,0:T(8,128)(2,1)}, u32[]{:S(2)}) copy-start(bf16[64,128]{1,0:T(8,128)(2,1)} %w_out.1) | copy-start | bytes 49156
  49.5 25.4 %copy-start.2 = (f32[64]{0:T(128)S(1)}, f32[64]{0:T(128)}, u32[]{:S(2)}) copy-start(f32[64]{0:T(128)} %gain.1) | copy-start | bytes 772
  49.5 25.4 %copy-start.3 = (f32[64]{0:T(128)S(1)}, f32[64]{0:T(128)}, u32[]{:S(2)}) copy-start(f32[64]{0:T(128)} %bias.1) | copy-start | bytes 772
  50.5 24.4 %copy-start = (bf16[64,128,128]{2,1,0:T(8,128)(2,1)S(1)}, bf16[64,128,128]{2,1,0:T(8,128)(2,1)}, u32[]{:S(2)}) copy-start(bf16[64,128,128]{2,1,0:T(8,128)(2,1)} %gate.1.gates) | copy-start | bytes 6291460

commit v6 on v5

--- a/solution.py
+++ b/solution.py
@@ -45,7 +45,9 @@
     small = copies(
         [(gain, affine.at[0:1]), (bias, affine.at[1:2]), (w_proj, loaded.at[0]), (w_gate, loaded.at[1])], sems
     )
-    large = chunks(pair, held, held_sems)
+    starts = [0, STEP]
+    parts = [slice(first, end) for first, end in zip(starts, starts[1:] + [rows])]
+    large = copies([(pair.at[part], held.at[part]) for part in parts], held_sems)
     for copy in small + large:
         copy.start()
     for copy in small:
@@ -69,7 +71,8 @@
     spans = [slice(s, s + STEP) for s in range(0, rows, STEP)]
     writes = copies([(made.at[:, :, span], out.at[:, :, span]) for span in spans], out_sems)
     for s in range(0, rows, STEP):
-        large[s // STEP].wait()
+        if s in starts:
+            large[starts.index(s)].wait()
         y = [products(s + t) for t in range(0, STEP, 2)]
         for c in range(0, channels, 16):
             lead = jnp.stack([v[c : c + 16, h * cols : (h + 1) * cols] for v in y for h in range(2)], axis=0)

time: 78.4 us -> 77.9 us (level)
  no operation moved by 1% of the time
where the time goes in v6:
time: 77.9 us; the launch traced here: 77.6 us
  blocking collectives  24.3 us (31%)
  waiting for transfers between devices  23.9 us (31%)
  Pallas kernels  16.8 us (22%)
  starting transfers between devices  11.5 us (15%)
  local copies, waits for them, and re-layouts  1.08 us (1%)
    all_to_all x1, blocking collectives, local(): lax.all_to_all(mid(core, *own(core, chan), other), CHIPS, 0, 0, tiled=True)  24.3 us
    all_to_all x1, waiting for transfers between devices, local(): chan = lax.all_to_all(lead, CHIPS, 0, 0, tiled=True)  21.9 us
    all_to_all x1, starting transfers between devices, local(): chan = lax.all_to_all(lead, CHIPS, 0, 0, tiled=True)  11.5 us
    pallas_call x1, Pallas kernels, gate(): pl.pallas_call(gate_kernel, in_specs=[pl.BlockSpec(memory_space=pl.ANY)]...  6.45 us
    pallas_call x1, Pallas kernels, pre(): pl.pallas_call(pre_kernel, in_specs=[pl.BlockSpec(memory_space=pl.ANY)] *...  5.12 us
    pallas_call x1, Pallas kernels, post(): pl.pallas_call(post_kernel, in_specs=[pl.BlockSpec(memory_space=pltpu.VME...  3.28 us
    ppermute x1, waiting for transfers between devices, local(): other = lax.ppermute(chan[:, 1], 'core', [(0, 1), (1, 0)])  1.96 us
  transfers between devices with their start and end apart: 2, of which 2 were waited for; matrix products, arithmetic and copies ran while one was open for 0% of the time, Pallas kernels for 9%

profile of v6, /device:TPU:0, one launch (start us, length us, event | category | flops | bytes accessed | tf_op | source)
XLA Modules:
  0.0 77.6 jit_solution(3487499624928589687)
XLA Ops:
  0.0 5.1 %pre.1 = bf16[64,2,64,128]{3,2,1,0:T(8,128)(2,1)} custom-call(bf16[64,128,128]{2,1,0:T(8,128)(2,1)} %pair.3, f32[1,128]{1,0:T(1,128)} %bitcast.5, f32[1,128]{1,0:T(1,128)} %bitcast.7, bf16[128,128]{1,0:T(8,128)(2,1)} %w_proj.1, bf16[128,128]{1,0:T(8,128)(2,1)} %w_gate.1), custom_call_target="tpu_custom_call" | custom-call | flops 1073741824 | bytes 4194304 | tf_op jit(solution)/shard_map/pre/pallas_call | solution.py:88
  5.1 11.5 %all-to-all-start = ((bf16[64,2,64,128]{3,2,1,0:T(8,128)(2,1)}), bf16[64,2,64,128]{3,2,1,0:T(8,128)(2,1)S(1)}, u32[]{:S(2)}, u32[]{:S(2)}) async-start(bf16[64,2,64,128]{3,2,1,0:T(8,128)(2,1)} %pre.1), calls=%async_computation | async-start | bytes 4194304 | tf_op jit(solution)/shard_map/all_to_all | solution.py:291
  16.6 6.5 %gate.1.gates = bf16[64,128,128]{2,1,0:T(8,128)(2,1)} custom-call(bf16[64,128,128]{2,1,0:T(8,128)(2,1)} %pair.3, f32[1,128]{1,0:T(1,128)} %bitcast.6, f32[1,128]{1,0:T(1,128)} %bitcast.8, bf16[128,128]{1,0:T(8,128)(2,1)} %w_out_gate.1), custom_call_target="tpu_custom_call" | custom-call | flops 1073741824 | bytes 16777216 | tf_op jit(solution)/shard_map/gate/pallas_call | solution.py:130
  23.1 21.9 %all-to-all-done.chan = bf16[64,2,64,128]{3,2,1,0:T(8,128)(2,1)S(1)} async-done(((bf16[64,2,64,128]{3,2,1,0:T(8,128)(2,1)}), bf16[64,2,64,128]{3,2,1,0:T(8,128)(2,1)S(1)}, u32[]{:S(2)}, u32[]{:S(2)}) %all-to-all-start) | async-done | bytes 2097184 | tf_op jit(solution)/shard_map/all_to_all | solution.py:291
  45.0 1.1 %slice_bitcast_fusion = bf16[64,64,128]{2,1,0:T(8,128)(2,1)} fusion(bf16[64,2,64,128]{3,2,1,0:T(8,128)(2,1)S(1)} %all-to-all-done.chan), kind=kLoop, calls=%fused_computation | loop fusion | bytes 2097152 | tf_op jit(solution)/shard_map/squeeze | solution.py:293
  46.1 0.0 collective-permute-start
  46.1 0.9 %own.1 = (bf16[512,1024]{1,0:T(8,128)(2,1)S(1)}, bf16[64,64,128]{2,1,0:T(8,128)(2,1)S(1)}) custom-call(s32[1]{0:T(128)} %bitcast.core, bf16[64,2,64,128]{3,2,1,0:T(8,128)(2,1)S(1)} %all-to-all-done.chan), custom_call_target="tpu_custom_call" | custom-call | flops 536870912 | bytes 4194304 | tf_op jit(solution)/shard_map/own/pallas_call | solution.py:179
  47.0 2.0 %collective-permute-done.other = bf16[64,64,128]{2,1,0:T(8,128)(2,1)S(1)} collective-permute-done((bf16[64,64,128]{2,1,0:T(8,128)(2,1)}, bf16[64,64,128]{2,1,0:T(8,128)(2,1)S(1)}, u32[]{:S(2)}, u32[]{:S(2)}) %collective-permute-start) | collective-permute-done | bytes 1048608 | tf_op jit(solution)/shard_map/ppermute | solution.py:293
  49.0 0.0 copy-start.1
  49.0 0.0 copy-start.2
  49.0 0.0 copy-start.3
  49.0 1.0 %mid.1 = bf16[64,64,128]{2,1,0:T(8,128)(2,1)S(1)} custom-call(s32[1]{0:T(128)} %bitcast.core, bf16[512,1024]{1,0:T(8,128)(2,1)S(1)} %get-tuple-element.10.a_side, bf16[64,64,128]{2,1,0:T(8,128)(2,1)S(1)} %get-tuple-element.11.mine, bf16[64,64,128]{2,1,0:T(8,128)(2,1)S(1)} %collective-permute-done.other), custom_call_target="tpu_custom_call" | custom-call | flops 536870912 | bytes 4194304 | tf_op jit(solution)/shard_map/mid/pallas_call | solution.py:213
  50.0 0.0 copy-start
  50.0 24.3 %all_to_all.10.back = bf16[64,64,128]{2,1,0:T(8,128)(2,1)S(1)} all-to-all(bf16[64,64,128]{2,1,0:T(8,128)(2,1)S(1)} %mid.1), channel_id=1, replica_groups=mesh['xh'=2,'z'=4,'core'=2,'xl'=2,'y'=4] {'xh','z','y','xl'}, dimensions={0} | all-to-all | bytes 2097152 | tf_op jit(solution)/shard_map/all_to_all | solution.py:295
  74.3 0.0 copy-done.1
  74.3 0.0 copy-done.2
  74.3 0.0 copy-done.3
  74.3 0.0 copy-done
  74.3 3.3 %post.1 = bf16[64,128,128]{2,1,0:T(8,128)(2,1)} custom-call(bf16[64,64,128]{2,1,0:T(8,128)(2,1)S(1)} %all_to_all.10.back, bf16[64,128,128]{2,1,0:T(8,128)(2,1)S(1)} %copy-done, f32[64]{0:T(128)S(1)} %copy-done.2, f32[64]{0:T(128)S(1)} %copy-done.3, bf16[64,128]{1,0:T(8,128)(2,1)S(1)} %copy-done.1), custom_call_target="tpu_custom_call" | custom-call | flops 268435456 | bytes 5242880 | tf_op jit(solution)/shard_map/post/pallas_call | solution.py:269
Async XLA Ops:
  5.1 39.9 %all-to-all-start = ((bf16[64,2,64,128]{3,2,1,0:T(8,128)(2,1)}), bf16[64,2,64,128]{3,2,1,0:T(8,128)(2,1)S(1)}, u32[]{:S(2)}, u32[]{:S(2)}) async-start(bf16[64,2,64,128]{3,2,1,0:T(8,128)(2,1)} %pre.1), calls=%async_computation | async-start | bytes 4194304 | tf_op jit(solution)/shard_map/all_to_all | solution.py:291
  46.1 2.9 %collective-permute-start = (bf16[64,64,128]{2,1,0:T(8,128)(2,1)}, bf16[64,64,128]{2,1,0:T(8,128)(2,1)S(1)}, u32[]{:S(2)}, u32[]{:S(2)}) collective-permute-start(bf16[64,64,128]{2,1,0:T(8,128)(2,1)} %slice_bitcast_fusion), channel_id=1, source_target_pairs={{0,8},{8,0},{1,9},{9,1},{2,10},{10,2},{3,11},{11,3},{4,12},{12,4},... | collective-permute-start | bytes 3145736 | tf_op jit(solution)/shard_map/ppermute | solution.py:293
  49.0 25.4 %copy-start.1 = (bf16[64,128]{1,0:T(8,128)(2,1)S(1)}, bf16[64,128]{1,0:T(8,128)(2,1)}, u32[]{:S(2)}) copy-start(bf16[64,128]{1,0:T(8,128)(2,1)} %w_out.1) | copy-start | bytes 49156
  49.0 25.4 %copy-start.2 = (f32[64]{0:T(128)S(1)}, f32[64]{0:T(128)}, u32[]{:S(2)}) copy-start(f32[64]{0:T(128)} %gain.1) | copy-start | bytes 772
  49.0 25.4 %copy-start.3 = (f32[64]{0:T(128)S(1)}, f32[64]{0:T(128)}, u32[]{:S(2)}) copy-start(f32[64]{0:T(128)} %bias.1) | copy-start | bytes 772
  50.0 24.3 %copy-start = (bf16[64,128,128]{2,1,0:T(8,128)(2,1)S(1)}, bf16[64,128,128]{2,1,0:T(8,128)(2,1)}, u32[]{:S(2)}) copy-start(bf16[64,128,128]{2,1,0:T(8,128)(2,1)} %gate.1.gates) | copy-start | bytes 6291460
